TPU v7x, 512 devices: a whole 4x8x8 slice. The times are simulated.
512 devices in a mesh: ctx: 16 (over y, core), nbr: 8 (over z), tp: 4 (over x).
Axes of the slice: x: 4, y: 8, z: 8, core: 2. Of those that a mesh axis runs over, the one named last changes fastest.
Arguments:
- hidden: bfloat16 [32768, 4096], P(('ctx', 'nbr'), 'tp'), may hold values from -6 to 6
- queries: bfloat16 [32768, 2048], P(('ctx', 'nbr'), 'tp'), may hold values from -6 to 6
- key_weight_matrix: bfloat16 [768, 2048], P('ctx', 'tp'), may hold values from -0.21875 to 0.21875
- value_weight_matrix: bfloat16 [768, 2048], P('ctx', 'tp'), may hold values from -0.21875 to 0.21875
- w_out: bfloat16 [2048, 4096], P('ctx', 'tp'), may hold values from -0.125 to 0.125
- neighbour_embed: bfloat16 [1024, 128, 768], P(('ctx', 'nbr')), may hold values from -6 to 6
- neighbour_ids: int32 [1024, 128], P(('ctx', 'nbr')), may hold values from 0 to 127999, as said below
- neighbour_count: int32 [512], P(('ctx', 'nbr')), may hold values from 0 to 2, as said below
- slot_seq: int32 [128, 8], replicated, may hold values from 0 to 7, as said below
- cond_keys: bfloat16 [32768, 768], P(('ctx', 'nbr'), 'tp'), may hold values from -6 to 6
- cond_values: bfloat16 [32768, 768], P(('ctx', 'nbr'), 'tp'), may hold values from -6 to 6
- enc_gain: bfloat16 [768], replicated, may hold values from 0.5 to 1.5
- enc_query: bfloat16 [768, 768], P(None, 'tp'), may hold values from -0.21875 to 0.21875
- enc_out: bfloat16 [768, 768], P('tp'), may hold values from -0.21875 to 0.21875
- final_gain: bfloat16 [768], replicated, may hold values from 0.5 to 1.5
Outputs:
- output: bfloat16 [32768, 4096], P(('ctx', 'nbr'), 'tp')
Inputs may be any that keep to these rules, and one draw needn't show every extreme that they name: `neighbour_ids`: every neighbour's ids are nonzero up to a length of at least 32 tokens and 0 after it. `slot_seq`: each row is a permutation of 0 to 7. `neighbour_count`: the last stretch of every block of positions has at least one valid neighbour.
All inputs are finite; a program needn't handle non-finite values.
Results may differ from a plain program's by a relative error of at most 0.0075.
Values may be sent and summed in bfloat16 or wider, within the bound.
A program may use at most 64 MiB of HBM per device.

v0:
```python
import jax
import jax.numpy as jnp
from jax import lax
from jax.sharding import PartitionSpec as P

HEAD_WIDTH = 128
EHD = 64
STRETCH_TOKENS = 64
NEIGHBOUR_TOKENS = 128
NEIGHBOUR_COUNT = 2


EPSILON = 1e-06


def from_behind(block, axis, distance):
    devices = range(lax.axis_size(axis))
    route = [(i - distance, i) for i in devices if i - distance in devices]
    return lax.ppermute(block, axis, route)


def row_rscale(matrix):
    return lax.rsqrt(jnp.mean(matrix * matrix, axis=-1, keepdims=True) + EPSILON)


def masked_attend(query_rows, key_rows, value_rows, allowed, score_scale):
    scores = (
        jnp.einsum("bqhd,bkhd->bhqk", query_rows, key_rows, preferred_element_type=jnp.float32)
        * score_scale
    )
    allowed_map = allowed[:, None, None, :]
    highest = jnp.max(jnp.where(allowed_map, scores, -1e30), axis=-1, keepdims=True)
    raised = jnp.where(allowed_map, jnp.exp(scores - highest), 0.0)
    totals = jnp.sum(raised, axis=-1, keepdims=True)
    anyone = jnp.any(allowed, axis=-1)[:, None, None, None]
    weights = (raised / jnp.where(anyone, totals, 1.0)).astype(jnp.bfloat16)
    return jnp.einsum(
        "bhqk,bkhd->bqhd", weights, value_rows, preferred_element_type=jnp.float32
    ).astype(jnp.bfloat16)


def per_device(
    hidden,
    queries,
    key_weight_matrix,
    value_weight_matrix,
    w_out,
    neighbour_embed,
    neighbour_ids,
    neighbour_count,
    slot_seq,
    cond_keys,
    cond_values,
    enc_gain,
    enc_query,
    enc_out,
    final_gain,
):
    tok_rows = hidden.shape[0]
    head_cols = queries.shape[1]
    heads_here = head_cols // HEAD_WIDTH
    block_seqs = neighbour_embed.shape[0]
    enc_width = neighbour_embed.shape[2]
    enc_cols = enc_query.shape[1]
    owners = lax.axis_size("nbr")
    tp_count = lax.axis_size("tp")
    per_owner = block_seqs // owners
    group_size = tok_rows // STRETCH_TOKENS
    quarter = NEIGHBOUR_TOKENS // tp_count
    ctx_place = lax.axis_index("ctx")
    nbr_place = lax.axis_index("nbr")
    tp_place = lax.axis_index("tp")
    table = lax.dynamic_slice_in_dim(slot_seq, ctx_place * owners, owners, 0)
    my_row = lax.dynamic_index_in_dim(table, nbr_place, 0, keepdims=False)
    send_stretches = (my_row // NEIGHBOUR_COUNT).reshape(owners, per_owner)
    sent_keys = jnp.take(
        cond_keys.reshape(group_size, STRETCH_TOKENS, enc_cols), send_stretches, axis=0
    )
    sent_values = jnp.take(
        cond_values.reshape(group_size, STRETCH_TOKENS, enc_cols), send_stretches, axis=0
    )
    got_keys, got_values = (
        lax.all_to_all(sent_keys, "nbr", split_axis=0, concat_axis=0, tiled=True),
        lax.all_to_all(sent_values, "nbr", split_axis=0, concat_axis=0, tiled=True),
    )
    wide_embed = neighbour_embed.astype(jnp.float32)
    own_rows = lax.dynamic_slice_in_dim(wide_embed, tp_place * quarter, quarter, 1)
    gain_wide = enc_gain.astype(jnp.float32)
    heads_enc = enc_cols // EHD
    normed = (wide_embed * row_rscale(wide_embed) * gain_wide).astype(jnp.bfloat16)
    enc_q = jnp.dot(
        normed.reshape(block_seqs * NEIGHBOUR_TOKENS, enc_width),
        enc_query,
        preferred_element_type=jnp.float32,
    ).astype(jnp.bfloat16)
    enc_q = enc_q.reshape(block_seqs, NEIGHBOUR_TOKENS, heads_enc, EHD)
    key_rows = got_keys.reshape(block_seqs, STRETCH_TOKENS, heads_enc, EHD)
    value_rows = got_values.reshape(block_seqs, STRETCH_TOKENS, heads_enc, EHD)
    mixed = masked_attend(
        enc_q,
        key_rows,
        value_rows,
        jnp.ones((block_seqs, STRETCH_TOKENS), dtype=bool),
        EHD ** (-0.5),
    )
    ordered = (
        mixed.reshape(block_seqs, tp_count, quarter, enc_cols)
        .transpose(1, 0, 2, 3)
        .reshape(tp_count * block_seqs * quarter, enc_cols)
    )
    term = jnp.dot(ordered, enc_out, preferred_element_type=jnp.float32)
    summed = (
        lax.psum_scatter(term.astype(jnp.bfloat16), "tp", scatter_dimension=0, tiled=True)
        .astype(jnp.float32)
        .reshape(block_seqs, quarter, enc_width)
    )
    updated = own_rows + summed
    encoded = (updated * row_rscale(updated) * final_gain.astype(jnp.float32)).astype(jnp.bfloat16)
    key_full, value_full = (
        lax.all_gather(key_weight_matrix, "ctx", axis=0, tiled=True),
        lax.all_gather(value_weight_matrix, "ctx", axis=0, tiled=True),
    )
    both_weights = jnp.concatenate([key_full, value_full], axis=1)
    back = lax.all_to_all(
        encoded.reshape(owners, per_owner, quarter, enc_width),
        "nbr",
        split_axis=0,
        concat_axis=0,
        tiled=True,
    )
    slot_kv = jnp.dot(
        lax.all_gather(back.reshape(block_seqs, quarter, enc_width), "tp", axis=1, tiled=True),
        both_weights,
        preferred_element_type=jnp.float32,
    ).astype(jnp.bfloat16)
    matches = my_row[:, None] == jnp.arange(block_seqs, dtype=jnp.int32)[None, :]
    inverse = jnp.sum(
        jnp.where(matches, jnp.arange(block_seqs, dtype=jnp.int32)[:, None], 0), axis=0
    )
    stretch_kv = jnp.take(slot_kv, inverse, axis=0).reshape(
        group_size, NEIGHBOUR_COUNT * NEIGHBOUR_TOKENS, 2 * head_cols
    )
    live = (
        jnp.arange(NEIGHBOUR_COUNT, dtype=jnp.int32)[None, :, None] < neighbour_count[:, None, None]
    ) & (neighbour_ids.reshape(group_size, NEIGHBOUR_COUNT, NEIGHBOUR_TOKENS) != 0)
    stretch_live = live.reshape(group_size, NEIGHBOUR_COUNT * NEIGHBOUR_TOKENS)

    def split_keys(kv_block):
        return kv_block[..., :head_cols].reshape(
            kv_block.shape[0], NEIGHBOUR_COUNT * NEIGHBOUR_TOKENS, heads_here, HEAD_WIDTH
        )

    def split_values(kv_block):
        return kv_block[..., head_cols:].reshape(
            kv_block.shape[0], NEIGHBOUR_COUNT * NEIGHBOUR_TOKENS, heads_here, HEAD_WIDTH
        )

    score_scale = HEAD_WIDTH ** (-0.5)
    live_mark = stretch_live.astype(jnp.bfloat16)
    before_kv, before_mark = from_behind(
        (stretch_kv[group_size - 1 :], live_mark[group_size - 1 :]), ("ctx", "nbr"), 1
    )
    then_kv = jnp.concatenate([before_kv, stretch_kv[:-1]], axis=0)
    then_live = jnp.concatenate([before_mark > 0.5, stretch_live[:-1]], axis=0)
    grouped = queries.reshape(group_size, STRETCH_TOKENS, heads_here, HEAD_WIDTH)
    early_rows = masked_attend(
        grouped[:, : STRETCH_TOKENS - 1],
        split_keys(then_kv),
        split_values(then_kv),
        then_live,
        score_scale,
    )
    last_rows = masked_attend(
        grouped[:, STRETCH_TOKENS - 1 :],
        split_keys(stretch_kv),
        split_values(stretch_kv),
        stretch_live,
        score_scale,
    )
    attended = jnp.concatenate([early_rows, last_rows], axis=1).reshape(tok_rows, head_cols)
    all_heads = lax.all_gather(attended, "tp", axis=1, tiled=True)
    mixed_out = jnp.dot(
        all_heads,
        lax.all_gather(w_out, "ctx", axis=0, tiled=True),
        preferred_element_type=jnp.float32,
    )
    return (hidden.astype(jnp.float32) + mixed_out).astype(jnp.bfloat16)


def solution(mesh):
    in_specs = (
        P(("ctx", "nbr"), "tp"),
        P(("ctx", "nbr"), "tp"),
        P("ctx", "tp"),
        P("ctx", "tp"),
        P("ctx", "tp"),
        P(("ctx", "nbr"), None, None),
        P(("ctx", "nbr"), None),
        P(("ctx", "nbr")),
        P(),
        P(("ctx", "nbr"), "tp"),
        P(("ctx", "nbr"), "tp"),
        P(),
        P(None, "tp"),
        P("tp", None),
        P(),
    )
    out_specs = P(("ctx", "nbr"), "tp")
    return jax.shard_map(
        per_device, mesh=mesh, in_specs=in_specs, out_specs=out_specs, check_vma=False
    )
```

profile of v0, /device:TPU:1, one launch (start us, length us, event | category | flops | bytes accessed | tf_op | source)
XLA Modules:
  0.0 219.3 jit_solution(40663971459019656)
XLA Ops:
  6.5 1.0 dynamic-slice_reduce_fusion
  7.6 1.0 copy.52
  8.6 1.0 copy.55
  10.7 0.9 fusion.37
  11.7 10.9 %all-to-all-start.1 = ((bf16[8,1,64,192]{3,2,1,0:T(8,128)(2,1)}), bf16[8,1,64,192]{3,2,1,0:T(8,128)(2,1)S(1)}, u32[]{:S(2)}, u32[]{:S(2)}) async-start(bf16[8,1,64,192]{3,2,1,0:T(8,128)(2,1)} %get-tuple-element.14), calls=%async_computation.1 | async-start | bytes 524288 | tf_op jit(solution)/shard_map/all_to_all | solution.py:83
  24.2 8.7 %all-to-all-done.1 = bf16[8,1,64,192]{3,2,1,0:T(8,128)(2,1)S(1)} async-done(((bf16[8,1,64,192]{3,2,1,0:T(8,128)(2,1)}), bf16[8,1,64,192]{3,2,1,0:T(8,128)(2,1)S(1)}, u32[]{:S(2)}, u32[]{:S(2)}) %all-to-all-start.1) | async-done | bytes 196640 | tf_op jit(solution)/shard_map/all_to_all | solution.py:83
  32.9 3.4 %all-to-all-start = ((bf16[8,1,64,192]{3,2,1,0:T(8,128)(2,1)}), bf16[8,1,64,192]{3,2,1,0:T(8,128)(2,1)S(1)}, u32[]{:S(2)}, u32[]{:S(2)}) async-start(bf16[8,1,64,192]{3,2,1,0:T(8,128)(2,1)} %get-tuple-element.15), calls=%async_computation | async-start | bytes 524288 | tf_op jit(solution)/shard_map/all_to_all | solution.py:84
  37.0 1.2 convolution_multiply_fusion.1
  38.2 7.4 %all-to-all-done = bf16[8,1,64,192]{3,2,1,0:T(8,128)(2,1)S(1)} async-done(((bf16[8,1,64,192]{3,2,1,0:T(8,128)(2,1)}), bf16[8,1,64,192]{3,2,1,0:T(8,128)(2,1)S(1)}, u32[]{:S(2)}, u32[]{:S(2)}) %all-to-all-start) | async-done | bytes 196640 | tf_op jit(solution)/shard_map/all_to_all | solution.py:84
  45.9 1.7 fusion.21
  49.0 1.7 convolution_convert_fusion.1
  50.8 2.0 convert_element_type.61
  52.7 27.2 %reduce-scatter.2.cloned.1.call-done = bf16[256,768]{1,0:T(8,128)(2,1)} async-done(((bf16[1024,768]{1,0:T(8,128)(2,1)}), bf16[256,768]{1,0:T(8,128)(2,1)}) %reduce-scatter.2.cloned.1.call-update) | async-done | bytes 393232 | tf_op jit(solution)/shard_map/reduce_scatter | solution.py:113
  79.9 1.5 multiply_reduce_fusion.1
  81.4 1.4 fusion.33
  82.8 18.6 %all_to_all.15 = bf16[8,1,32,768]{3,2,1,0:T(8,128)(2,1)} all-to-all(bf16[8,1,32,768]{3,2,1,0:T(8,128)(2,1)S(1)} %fusion.33), channel_id=1, replica_groups=mesh['ctx'=16,'nbr'=8,'tp'=4] {'nbr'}, dimensions={0} | all-to-all | bytes 786432 | tf_op jit(solution)/shard_map/all_to_all | solution.py:124
  102.7 2.2 %collective-permute-start.1 = (bf16[1,256]{1,0:T(2,128)(2,1)S(1)}, bf16[1,256]{1,0:T(2,128)(2,1)S(1)}, u32[]{:S(2)}, u32[]{:S(2)}) collective-permute-start(bf16[1,256]{1,0:T(2,128)(2,1)S(1)} %slice_convert_fusion), channel_id=1, source_target_pairs={{0,4},{4,8},{8,12},{12,16},{16,20},{20,24},{24,28},{28,32},{32,36}... | collective-permute-start | bytes 1544 | tf_op jit(solution)/shard_map/ppermute | solution.py:19
  105.5 23.3 %all_gather.16 = bf16[768,512]{1,0:T(8,128)(2,1)S(1)} all-gather(bf16[48,512]{1,0:T(8,128)(2,1)S(1)} %copy-done.7), channel_id=1, replica_groups=mesh['ctx'=16,'nbr'=8,'tp'=4] {'ctx'}, dimensions={0}, use_global_device_ids=true | all-gather | bytes 835584 | tf_op jit(solution)/shard_map/all_gather | solution.py:120
  128.8 17.3 %all_gather.17 = bf16[768,512]{1,0:T(8,128)(2,1)S(1)} all-gather(bf16[48,512]{1,0:T(8,128)(2,1)S(1)} %copy-done.8), channel_id=1, replica_groups=mesh['ctx'=16,'nbr'=8,'tp'=4] {'ctx'}, dimensions={0}, use_global_device_ids=true | all-gather | bytes 835584 | tf_op jit(solution)/shard_map/all_gather | solution.py:121
  146.5 4.5 %convolution_convert_fusion = bf16[8,128,1024]{2,1,0:T(8,128)(2,1)} fusion(bf16[768,512]{1,0:T(8,128)(2,1)S(1)} %all_gather.17, bf16[768,512]{1,0:T(8,128)(2,1)S(1)} %all_gather.16, bf16[8,1,128,768]{3,2,0,1:T(8,128)(2,1)} %all-gather.9.cloned.1.call-done), kind=kOutput, calls=%fused_computation.12 | convolution fusion | flops 1614807040 | bytes 5242880 | tf_op jit(solution)/shard_map/dot_general | solution.py:131
  151.0 2.3 %gather_fusion = bf16[8,128,1024]{2,1,0:T(8,128)(2,1)S(1)} fusion(bf16[8,128,1024]{2,1,0:T(8,128)(2,1)} %convolution_convert_fusion, s32[1024]{0:T(1024)S(1)} %pad_clamp_fusion), kind=kCustom, calls=%fused_computation.2 | custom fusion | bytes 4194336 | tf_op jit(solution)/shard_map/jit(_take)/gather | solution.py:140
  153.6 1.3 copy-done.2
  154.9 1.0 copy.63
  155.9 2.1 collective-permute-start
  158.3 1.3 slice_bitcast_fusion
  161.7 1.5 copy.80
  163.6 6.0 %collective-permute-done = bf16[1,256,1024]{1,2,0:T(8,128)(2,1)} collective-permute-done((bf16[1,256,1024]{1,2,0:T(8,128)(2,1)}, bf16[1,256,1024]{1,2,0:T(8,128)(2,1)}, u32[]{:S(2)}, u32[]{:S(2)}) %collective-permute-start) | collective-permute-done | bytes 524320 | tf_op jit(solution)/shard_map/ppermute | solution.py:19
  169.5 2.1 pad_maximum_fusion
  172.9 1.8 fusion.22
  175.8 3.3 %all-gather.7.cloned.1.call-done = bf16[2048,1024]{1,0:T(8,128)(2,1)} async-done(((bf16[128,1024]{1,0:T(8,128)(2,1)}), bf16[2048,1024]{1,0:T(8,128)(2,1)}) %all-gather.7.cloned.1.call-update) | async-done | bytes 4194320 | tf_op jit(solution)/shard_map/all_gather | solution.py:184
  179.1 29.1 %all-gather.5.cloned.1.call-done = bf16[256,2048]{1,0:T(8,128)(2,1)} async-done(((bf16[256,512]{1,0:T(8,128)(2,1)}), bf16[256,2048]{1,0:T(8,128)(2,1)}) %all-gather.5.cloned.1.call-update) | async-done | bytes 1048592 | tf_op jit(solution)/shard_map/all_gather | solution.py:181
  208.2 4.6 %fusion.18 = bf16[256,1024]{1,0:T(8,128)(2,1)} fusion(bf16[256,2048]{1,0:T(8,128)(2,1)} %all-gather.5.cloned.1.call-done, bf16[2048,1024]{1,0:T(8,128)(2,1)} %all-gather.7.cloned.1.call-done, bf16[256,1024]{1,0:T(8,128)(2,1)S(1)} %copy-done.12), kind=kOutput, calls=%fused_computation.27 | convolution fusion | flops 1074528256 | bytes 6291456 | tf_op jit(solution)/shard_map/dot_general | solution.py:182
  (101 shorter events, 12.7 us)
Async XLA Ops:
  6.5 42.4 %copy-start = (bf16[192,768]{1,0:T(8,128)(2,1)S(1)}, bf16[192,768]{1,0:T(8,128)(2,1)}, u32[]{:S(2)}) copy-start(bf16[192,768]{1,0:T(8,128)(2,1)} %param.30) | copy-start | bytes 884740
  6.5 16.0 %copy-start.1 = (bf16[8,128,768]{2,1,0:T(8,128)(2,1)S(1)}, bf16[8,128,768]{2,1,0:T(8,128)(2,1)}, u32[]{:S(2)}) copy-start(bf16[8,128,768]{2,1,0:T(8,128)(2,1)} %param.22) | copy-start | bytes 4718596
  9.6 13.3 %copy-start.10 = (bf16[768]{0:T(1024)(128)(2,1)S(1)}, bf16[768]{0:T(1024)(128)(2,1)}, u32[]{:S(2)}) copy-start(bf16[768]{0:T(1024)(128)(2,1)} %param.28) | copy-start | bytes 4612
  11.7 21.2 %all-to-all-start.1 = ((bf16[8,1,64,192]{3,2,1,0:T(8,128)(2,1)}), bf16[8,1,64,192]{3,2,1,0:T(8,128)(2,1)S(1)}, u32[]{:S(2)}, u32[]{:S(2)}) async-start(bf16[8,1,64,192]{3,2,1,0:T(8,128)(2,1)} %get-tuple-element.14), calls=%async_computation.1 | async-start | bytes 524288 | tf_op jit(solution)/shard_map/all_to_all | solution.py:83
  22.5 1.0 copy-start.5
  32.9 12.8 %all-to-all-start = ((bf16[8,1,64,192]{3,2,1,0:T(8,128)(2,1)}), bf16[8,1,64,192]{3,2,1,0:T(8,128)(2,1)S(1)}, u32[]{:S(2)}, u32[]{:S(2)}) async-start(bf16[8,1,64,192]{3,2,1,0:T(8,128)(2,1)} %get-tuple-element.15), calls=%async_computation | async-start | bytes 524288 | tf_op jit(solution)/shard_map/all_to_all | solution.py:84
  36.3 43.6 %reduce-scatter.2.cloned.1.call-start = ((), (), s32[]{:S(2)}) async-start(), calls=%async_computation.4 | async-start | bytes 1966080 | tf_op jit(solution)/shard_map/reduce_scatter | solution.py:113
  50.7 95.8 %all-gather.9.cloned.1.call-start = ((), (), s32[]{:S(2)}) async-start(), calls=%async_computation.7 | async-start | bytes 1966080 | tf_op jit(solution)/shard_map/all_gather | solution.py:132
  50.8 2.0 copy-start.11
  79.9 22.3 %copy-start.13 = (s32[4]{0:T(128)S(1)}, s32[4]{0:T(128)}, u32[]{:S(2)}) copy-start(s32[4]{0:T(128)} %param.24) | copy-start | bytes 52
  79.9 22.5 %copy-start.9 = (s32[8,128]{1,0:T(8,128)S(1)}, s32[8,128]{1,0:T(8,128)}, u32[]{:S(2)}) copy-start(s32[8,128]{1,0:T(8,128)} %param.23) | copy-start | bytes 12292
  79.9 25.0 %copy-start.6 = (bf16[256,512]{1,0:T(8,128)(2,1)S(1)}, bf16[256,512]{1,0:T(8,128)(2,1)}, u32[]{:S(2)}) copy-start(bf16[256,512]{1,0:T(8,128)(2,1)} %param.18) | copy-start | bytes 786436
  81.4 24.1 %copy-start.7 = (bf16[48,512]{1,0:T(8,128)(2,1)S(1)}, bf16[48,512]{1,0:T(8,128)(2,1)}, u32[]{:S(2)}) copy-start(bf16[48,512]{1,0:T(8,128)(2,1)} %param.19) | copy-start | bytes 147460
  81.4 47.3 %copy-start.8 = (bf16[48,512]{1,0:T(8,128)(2,1)S(1)}, bf16[48,512]{1,0:T(8,128)(2,1)}, u32[]{:S(2)}) copy-start(bf16[48,512]{1,0:T(8,128)(2,1)} %param.20) | copy-start | bytes 147460
  101.4 77.7 %all-gather.7.cloned.1.call-start = ((), (), s32[]{:S(2)}) async-start(), calls=%async_computation.6 | async-start | bytes 4456448 | tf_op jit(solution)/shard_map/all_gather | solution.py:184
  102.2 106.0 %all-gather.5.cloned.1.call-start = ((), (), s32[]{:S(2)}) async-start(), calls=%async_computation.5 | async-start | bytes 1310720 | tf_op jit(solution)/shard_map/all_gather | solution.py:181
  102.7 43.6 %collective-permute-start.1 = (bf16[1,256]{1,0:T(2,128)(2,1)S(1)}, bf16[1,256]{1,0:T(2,128)(2,1)S(1)}, u32[]{:S(2)}, u32[]{:S(2)}) collective-permute-start(bf16[1,256]{1,0:T(2,128)(2,1)S(1)} %slice_convert_fusion), channel_id=1, source_target_pairs={{0,4},{4,8},{8,12},{12,16},{16,20},{20,24},{24,28},{28,32},{32,36}... | collective-permute-start | bytes 1544 | tf_op jit(solution)/shard_map/ppermute | solution.py:19
  105.0 41.5 %copy-start.3 = (bf16[4,64,4,128]{3,2,1,0:T(4,128)(2,1)}, bf16[4,64,4,128]{3,2,1,0:T(4,128)(2,1)S(1)}, u32[]{:S(2)}) copy-start(bf16[4,64,4,128]{3,2,1,0:T(4,128)(2,1)S(1)} %reshape.317) | copy-start | bytes 786436
  153.6 1.3 copy-start.2
  155.9 13.6 %collective-permute-start = (bf16[1,256,1024]{1,2,0:T(8,128)(2,1)}, bf16[1,256,1024]{1,2,0:T(8,128)(2,1)}, u32[]{:S(2)}, u32[]{:S(2)}) collective-permute-start(bf16[1,256,1024]{1,2,0:T(8,128)(2,1)} %copy.63), channel_id=1, source_target_pairs={{0,4},{4,8},{8,12},{12,16},{16,20},{20,24},{24,28},{28,32},{32,36}... | collective-permute-start | bytes 1572872 | tf_op jit(solution)/shard_map/ppermute | solution.py:19
  159.6 1.4 slice-start
  163.6 8.1 %slice-start.1 = ((bf16[4,64,4,128]{3,2,1,0:T(4,128)(2,1)}), bf16[4,63,4,128]{3,2,1,0:T(4,128)(2,1)S(1)}, s32[]{:S(2)}) async-start(bf16[4,64,4,128]{3,2,1,0:T(4,128)(2,1)} %copy-done.3), calls=%async_computation.9 | async-start | bytes 516096 | tf_op jit(solution)/shard_map/slice | solution.py:167
  171.7 1.3 copy-start.4
  172.9 35.2 %copy-start.12 = (bf16[256,1024]{1,0:T(8,128)(2,1)S(1)}, bf16[256,1024]{1,0:T(8,128)(2,1)}, u32[]{:S(2)}) copy-start(bf16[256,1024]{1,0:T(8,128)(2,1)} %param.17) | copy-start | bytes 1572868
Sparse Core Ops, SparseCore 0:
  50.8 29.0 reduce-scatter.1
  101.6 30.1 all-gather.8
  133.9 45.1 all-gather.6
  181.1 27.0 all-gather.4
where the time goes:
time: 220 us; the launch traced here: 219 us
  waiting for transfers between devices  82.3 us (37%)
  blocking collectives  59.2 us (27%)
  starting transfers between devices  18.7 us (8%)
  matrix products  17.6 us (8%)
  local copies, waits for them, and re-layouts  17 us (8%)
  between operations  13.6 us (6%)
  other arithmetic  10.8 us (5%)
    all_gather x1, waiting for transfers between devices, per_device(): all_heads = lax.all_gather(attended, 'tp', axis=1, tiled=True)  29.1 us
    reduce_scatter x1, waiting for transfers between devices, per_device(): lax.psum_scatter(term.astype(jnp.bfloat16), 'tp', scatter_dimension=0, ti...  27.2 us
    all_gather x1, blocking collectives, per_device(): lax.all_gather(key_weight_matrix, 'ctx', axis=0, tiled=True)  23.3 us
    all_to_all x1, blocking collectives, per_device(): lax.all_to_all(encoded.reshape(owners, per_owner, quarter, enc_width), 'n...  18.6 us
    all_gather x1, blocking collectives, per_device(): lax.all_gather(value_weight_matrix, 'ctx', axis=0, tiled=True)  17.3 us
    all_to_all x1, starting transfers between devices, per_device(): lax.all_to_all(sent_keys, 'nbr', split_axis=0, concat_axis=0, tiled=True)  10.9 us
    all_to_all x1, waiting for transfers between devices, per_device(): lax.all_to_all(sent_keys, 'nbr', split_axis=0, concat_axis=0, tiled=True)  8.67 us
    all_to_all x1, waiting for transfers between devices, per_device(): lax.all_to_all(sent_values, 'nbr', split_axis=0, concat_axis=0, tiled=True)  7.43 us
  transfers between devices with their start and end apart: 8, of which 6 were waited for; matrix products, arithmetic and copies ran while one was open for 12% of the time, Pallas kernels for 0%

commit v1 on v0

v1 whole, which is shorter than its diff:
```python
import jax
import jax.numpy as jnp
from jax import lax
from jax.experimental import pallas as pl
from jax.experimental.pallas import tpu as pltpu
from jax.sharding import PartitionSpec as P

HEAD_WIDTH = 128
EHD = 64
STRETCH_TOKENS = 64
NEIGHBOUR_TOKENS = 128
EPSILON = 1e-06
MESH = pl.DeviceIdType.MESH
NT = (((1,), (1,)), ((), ()))
TN = (((0,), (0,)), ((), ()))
NN = (((1,), (0,)), ((), ()))

S_EMB, S_COND, S_ENC_W, S_KV_RIGHT, S_KV_LEFT, S_KV_MATE, S_MASK, S_AG, S_PREV, S_ATT = (
    0, 2, 5, 13, 17, 20, 21, 22, 28, 29,
)
N_SEMS = 35


def dot(a, b, dims):
    return lax.dot_general(a, b, dims, preferred_element_type=jnp.float32)


def norm_rows(rows, gain):
    scale = lax.rsqrt(jnp.mean(rows * rows, axis=-1, keepdims=True) + EPSILON)
    return (rows * scale * gain).astype(jnp.bfloat16)


def body(
    slots, counts, embed, cond_k_far, cond_v_far, enc_q, enc_o, key_w, value_w, queries_far, ids_far, gain_in, gain_out,
    attended,
    cond_k, cond_v, queries, ids,
    emb, packs, cond_send, cond, enc_w, normed, mixed, encoded, kv_w, keys, values,
    last_send, last_got, mask_send, mask_got, key_mask, partial, send, recv, local,
):
    c, n, t = lax.axis_index("ctx"), lax.axis_index("nbr"), lax.axis_index("tp")
    block = c * 8 + n
    right, left, across = lax.rem(t + 1, 4), lax.rem(t + 3, 4), lax.rem(t + 2, 4)
    core = lax.rem(c, 2)
    y = c // 2
    mate = c + 1 - 2 * core
    c_right, c_left = lax.rem(c + 2, 16), lax.rem(c + 14, 16)
    first = lax.rem(t - n + 8, 4)
    nxt = lax.rem(block + 1, 128)
    before = lax.rem(block + 127, 128)
    next_device = (nxt // 8, lax.rem(nxt, 8), t)
    before_device = (before // 8, lax.rem(before, 8), t)

    def copy(src, dst, s, r, device):
        return pltpu.make_async_remote_copy(
            src_ref=src, dst_ref=dst, send_sem=send.at[s], recv_sem=recv.at[r],
            device_id=device, device_id_type=MESH,
        )

    def to(ref, s, device, dst=None, r=None):
        made = copy(ref, ref if dst is None else dst, s, s if r is None else r, device)
        made.start()
        sent.append(made)

    def arrived(ref, r):
        copy(ref, ref, r, r, (c, n, right)).wait_recv()

    sent = []

    own = [
        pltpu.make_async_copy(enc_q, enc_w.at[0, t], local.at[0]),
        pltpu.make_async_copy(enc_o, enc_w.at[1, t], local.at[1]),
        pltpu.make_async_copy(key_w, kv_w.at[0, y, core], local.at[2]),
        pltpu.make_async_copy(value_w, kv_w.at[1, y, core], local.at[3]),
        pltpu.make_async_copy(cond_k_far, cond_k, local.at[5]),
        pltpu.make_async_copy(cond_v_far, cond_v, local.at[6]),
        pltpu.make_async_copy(queries_far, queries, local.at[7]),
        pltpu.make_async_copy(ids_far, ids, local.at[8]),
    ]
    for made in own:
        made.start()

    barrier = pltpu.get_barrier_semaphore()
    for device in (
        (c, n, right), (c, n, left), (c, n, across), (mate, n, t), (c_right, n, t), (c_left, n, t), before_device,
    ):
        pl.semaphore_signal(barrier, inc=1, device_id=device, device_id_type=MESH)
    for k in range(2):
        other = first + 4 * k

        @pl.when(other != n)
        def _():
            pl.semaphore_signal(barrier, inc=1, device_id=(c, other, t), device_id_type=MESH)

    with_self = jnp.where(lax.rem(2 * n, 4) == t, 1, 0)
    pl.semaphore_wait(barrier, 9 - with_self)

    mine = n // 4

    def emb_copy(k):
        other = first + 4 * k
        return copy(embed.at[other], emb.at[mine], S_EMB + k, S_EMB + mine, (c, other, t))

    for k in range(2):
        other = first + 4 * k

        @pl.when(other != n)
        def _():
            emb_copy(k).start()

        @pl.when(other == n)
        def _():
            pltpu.make_async_copy(embed.at[n], emb.at[mine], local.at[4]).start()

    own[0].wait()
    own[1].wait()
    to(enc_w.at[:, t, core], S_ENC_W, (c, n, right))
    to(enc_w.at[:, t, core], S_ENC_W + 1, (c, n, left))

    own[4].wait()
    own[5].wait()
    for st in range(4):
        at = slice(st * STRETCH_TOKENS, (st + 1) * STRETCH_TOKENS)
        packs[st] = jnp.concatenate([cond_k[:, at], cond_v[:, at]], axis=1)
    for d in (1, 3, 2):
        target = lax.rem(t + d, 4)
        start = lax.rem(target - n + 8, 4)
        for k in range(2):
            cond_send[d - 1, k] = packs[slots[start + 4 * k, block] // 2]
        to(cond_send.at[d - 1], S_COND + d - 1, (c, n, target), dst=cond.at[t])
    for k in range(2):
        cond[t, k] = packs[slots[first + 4 * k, block] // 2]

    own[2].wait()
    own[3].wait()

    def kv_right(s):
        to(kv_w.at[:, lax.rem(y - s + 8, 8), core], S_KV_RIGHT + s, (c_right, n, t))

    def kv_left(s):
        to(kv_w.at[:, lax.rem(y + s, 8), core], S_KV_LEFT + s, (c_left, n, t))

    def kv_right_in(s):
        arrived(kv_w.at[:, lax.rem(y - s - 1 + 8, 8), core], S_KV_RIGHT + s)

    def kv_left_in(s):
        arrived(kv_w.at[:, lax.rem(y + s + 1, 8), core], S_KV_LEFT + s)

    kv_right(0)
    kv_left(0)

    own[7].wait()
    row = lax.broadcasted_iota(jnp.int32, (8, 128), 0)
    count = jnp.zeros((8, 128), jnp.int32)
    for st in range(4):
        count = jnp.where(row // 2 == st, counts[st], count)
    mask_send[...] = jnp.where((lax.rem(row, 2) < count) & (ids[...] != 0), 1.0, 0.0)
    to(mask_send, S_MASK, next_device, dst=mask_got)
    mask = mask_send[...]
    for s in range(8):
        key_mask[s] = jnp.broadcast_to(mask[s : s + 1], (128, 128)).T

    for k in range(2):
        other = first + 4 * k

        @pl.when(other != n)
        def _():
            arrived(emb.at[k], S_EMB + k)

        @pl.when(other == n)
        def _():
            pltpu.make_async_copy(embed.at[n], emb.at[k], local.at[4]).wait()

        normed[k] = norm_rows(emb[k].astype(jnp.float32), gain_in[...].astype(jnp.float32))

    def encode_heads(shard):
        query = dot(enc_w[0, shard].reshape(192, 768), normed[...].reshape(256, 768), NT)
        query = query.astype(jnp.bfloat16) * jnp.bfloat16(EHD ** (-0.5))
        columns = []
        for k in range(2):
            rows = []
            for h in range(3):
                at = slice(h * EHD, (h + 1) * EHD)
                both = cond[shard, k, at, :]
                scores = dot(both, query[at, k * 128 : (k + 1) * 128], TN)[:STRETCH_TOKENS]
                raised = jnp.exp(scores - jnp.max(scores, axis=0, keepdims=True))
                weights = (raised / jnp.sum(raised, axis=0, keepdims=True)).astype(jnp.bfloat16)
                spread = jnp.concatenate([jnp.zeros_like(weights), weights], axis=0)
                rows.append(dot(both, spread, NN).astype(jnp.bfloat16))
            columns.append(jnp.concatenate(rows, axis=0))
        mixed[shard] = jnp.concatenate(columns, axis=1)

    encode_heads(t)

    kv_right_in(0)
    kv_right(1)
    kv_left_in(0)
    kv_left(1)

    arrived(enc_w.at[:, left, core], S_ENC_W)
    to(enc_w.at[0, left, core], S_ENC_W + 2, (c, n, right))
    to(enc_w.at[:, left, core], S_ENC_W + 4, (mate, n, t))
    arrived(enc_w.at[:, right, core], S_ENC_W + 1)
    to(enc_w.at[1, right, core], S_ENC_W + 3, (c, n, left))
    to(enc_w.at[:, right, core], S_ENC_W + 5, (mate, n, t))
    arrived(cond.at[left], S_COND)
    arrived(enc_w.at[:, left, 1 - core], S_ENC_W + 4)
    encode_heads(left)
    kv_right_in(1)
    kv_right(2)
    kv_left_in(1)
    kv_left(2)
    arrived(enc_w.at[0, across, core], S_ENC_W + 2)
    to(enc_w.at[0, across, core], S_ENC_W + 6, (mate, n, t))
    arrived(enc_w.at[1, across, core], S_ENC_W + 3)
    to(enc_w.at[1, across, core], S_ENC_W + 7, (mate, n, t))
    arrived(cond.at[right], S_COND + 2)
    arrived(enc_w.at[:, right, 1 - core], S_ENC_W + 5)
    encode_heads(right)
    kv_right_in(2)
    kv_right(3)
    arrived(cond.at[across], S_COND + 1)
    arrived(enc_w.at[0, across, 1 - core], S_ENC_W + 6)
    encode_heads(across)
    arrived(enc_w.at[1, across, 1 - core], S_ENC_W + 7)

    updated = dot(mixed[...].reshape(768, 256), enc_w[1].reshape(768, 768), TN)
    gain = gain_out[...].astype(jnp.float32)
    for k in range(2):
        rows = emb[k].astype(jnp.float32) + updated[k * 128 : (k + 1) * 128]
        encoded[first + 4 * k] = norm_rows(rows, gain)

    for k in range(2):
        to(encoded.at[first + 4 * k], S_AG + 2 * k, (c, n, right))
        to(encoded.at[first + 4 * k], S_AG + 2 * k + 1, (c, n, left))

    kv_left_in(2)
    kv_right_in(3)
    to(kv_w.at[:, :, core], S_KV_MATE, (mate, n, t))
    arrived(kv_w.at[:, :, 1 - core], S_KV_MATE)

    def project(rows):
        made = []
        for i in range(2):
            made.append(dot(rows, kv_w[i].reshape(768, 512), NN).astype(jnp.bfloat16))
        return made

    def project_pair(start):
        rows = jnp.concatenate([encoded[start], encoded[start + 4]], axis=0)
        got_k, got_v = project(rows)
        for k in range(2):
            keys[start + 4 * k] = got_k[k * 128 : (k + 1) * 128]
            values[start + 4 * k] = got_v[k * 128 : (k + 1) * 128]

    def first_of(shard):
        return lax.rem(shard - n + 8, 4)

    project_pair(first)
    arrived(encoded.at[first_of(left)], S_AG)
    to(encoded.at[first_of(left)], S_AG + 4, (c, n, right))
    arrived(encoded.at[first_of(right) + 4], S_AG + 3)
    to(encoded.at[first_of(right) + 4], S_AG + 5, (c, n, left))
    arrived(encoded.at[first_of(left) + 4], S_AG + 2)
    project_pair(first_of(left))
    arrived(encoded.at[first_of(right)], S_AG + 1)
    project_pair(first_of(right))
    arrived(encoded.at[first_of(across)], S_AG + 4)
    arrived(encoded.at[first_of(across) + 4], S_AG + 5)

    slot_of = []
    for s in range(8):
        place = jnp.int32(0)
        for o in range(1, 8):
            place = jnp.where(slots[o, block] == s, o, place)
        slot_of.append(place)
    for k in range(2):
        last_send[k] = encoded[slot_of[6 + k]]
    to(last_send, S_PREV, next_device, dst=last_got)
    project_pair(first_of(across))

    own[6].wait()
    lane = lax.broadcasted_iota(jnp.int32, (1, 128), 1)

    def attend(key_rows, value_rows, allowed, h, start, low, high):
        at = slice(h * HEAD_WIDTH, (h + 1) * HEAD_WIDTH)
        scores = dot(key_rows, queries[start : start + 128, at], NT) * HEAD_WIDTH ** (-0.5)
        scores = jnp.where(allowed > 0, scores, -1e30)
        raised = jnp.exp(scores - jnp.max(scores, axis=0, keepdims=True)) * allowed
        total = jnp.sum(raised, axis=0, keepdims=True)
        use = (total > 0) & (lane >= low) & (lane < high)
        share = jnp.where(use, 1.0 / jnp.where(use, total, 1.0), 0.0)
        return dot((raised * share).astype(jnp.bfloat16), value_rows, TN)

    def stretch_attend(st, h, start, low, high):
        at = slice(h * HEAD_WIDTH, (h + 1) * HEAD_WIDTH)
        pair = (slot_of[2 * st], slot_of[2 * st + 1])
        key_rows = jnp.concatenate([keys[p, :, at] for p in pair], axis=0)
        value_rows = jnp.concatenate([values[p, :, at] for p in pair], axis=0)
        allowed = key_mask[2 * st : 2 * st + 2].reshape(256, 128)
        return attend(key_rows, value_rows, allowed, h, start, low, high)

    for h in range(4):
        at = slice(h * HEAD_WIDTH, (h + 1) * HEAD_WIDTH)
        one = stretch_attend(0, h, 0, 63, 127)
        two = stretch_attend(1, h, 64, 63, 127)
        three = stretch_attend(2, h, 128, 63, 127)
        four = stretch_attend(3, h, 128, 127, 128)
        partial[:, at] = jnp.concatenate([one[:64], one[64:] + two[:64]], axis=0)
        lower = jnp.concatenate([two[64:] + three[:64] + four[:64], three[64:] + four[64:]], axis=0)
        attended[128:256, pl.ds(pl.multiple_of(t * 512 + h * 128, 128), 128)] = lower.astype(jnp.bfloat16)

    def piece(half, shard):
        return attended.at[pl.ds(128 * half, 128), pl.ds(pl.multiple_of(shard * 512, 512), 512)]

    to(piece(1, t), S_ATT, (c, n, right))
    to(piece(1, t), S_ATT + 1, (c, n, left))

    arrived(mask_got, S_MASK)
    seen = mask_got[...] * jnp.where(block > 0, 1.0, 0.0)
    allowed = jnp.concatenate(
        [jnp.broadcast_to(seen[6 + k : 7 + k], (128, 128)).T for k in range(2)], axis=0
    )
    arrived(last_got, S_PREV)
    got_k, got_v = project(last_got[...].reshape(256, 768))
    for h in range(4):
        at = slice(h * HEAD_WIDTH, (h + 1) * HEAD_WIDTH)
        upper = partial[:, at] + attend(got_k[:, at], got_v[:, at], allowed, h, 0, 0, 63)
        attended[0:128, pl.ds(pl.multiple_of(t * 512 + h * 128, 128), 128)] = upper.astype(jnp.bfloat16)

    to(piece(0, t), S_ATT + 2, (c, n, right))
    to(piece(0, t), S_ATT + 3, (c, n, left))
    arrived(piece(1, left), S_ATT)
    to(piece(1, left), S_ATT + 4, (c, n, right))
    arrived(piece(0, right), S_ATT + 3)
    to(piece(0, right), S_ATT + 5, (c, n, left))
    arrived(piece(1, right), S_ATT + 1)
    arrived(piece(0, left), S_ATT + 2)
    arrived(piece(1, across), S_ATT + 4)
    arrived(piece(0, across), S_ATT + 5)

    for k in range(2):

        @pl.when(first + 4 * k != n)
        def _():
            emb_copy(k).wait_send()

    for made in sent:
        made.wait_send()


def per_device(
    hidden,
    queries,
    key_weight_matrix,
    value_weight_matrix,
    w_out,
    neighbour_embed,
    neighbour_ids,
    neighbour_count,
    slot_seq,
    cond_keys,
    cond_values,
    enc_gain,
    enc_query,
    enc_out,
    final_gain,
):
    out_rows = lax.all_gather(w_out, "ctx", axis=0, tiled=True)
    vmem, hbm = pl.BlockSpec(memory_space=pltpu.VMEM), pl.BlockSpec(memory_space=pltpu.HBM)
    smem = pl.BlockSpec(memory_space=pltpu.SMEM)
    bf16, f32 = jnp.bfloat16, jnp.float32
    attended = pl.pallas_call(
        body,
        out_shape=jax.ShapeDtypeStruct((256, 2048), bf16),
        in_specs=[smem, smem, *[hbm] * 9, vmem, vmem],
        out_specs=vmem,
        scratch_shapes=[
            pltpu.VMEM((192, 256), bf16),
            pltpu.VMEM((192, 256), bf16),
            pltpu.VMEM((256, 512), bf16),
            pltpu.VMEM((8, 128), jnp.int32),
            pltpu.VMEM((2, 128, 768), bf16),
            pltpu.VMEM((4, 192, 128), bf16),
            pltpu.VMEM((3, 2, 192, 128), bf16),
            pltpu.VMEM((4, 2, 192, 128), bf16),
            pltpu.VMEM((2, 4, 2, 96, 768), bf16),
            pltpu.VMEM((2, 128, 768), bf16),
            pltpu.VMEM((4, 192, 256), bf16),
            pltpu.VMEM((8, 128, 768), bf16),
            pltpu.VMEM((2, 8, 2, 48, 512), bf16),
            pltpu.VMEM((8, 128, 512), bf16),
            pltpu.VMEM((8, 128, 512), bf16),
            pltpu.VMEM((2, 128, 768), bf16),
            pltpu.VMEM((2, 128, 768), bf16),
            pltpu.VMEM((8, 128), f32),
            pltpu.VMEM((8, 128), f32),
            pltpu.VMEM((8, 128, 128), f32),
            pltpu.VMEM((128, 512), f32),
            pltpu.SemaphoreType.DMA((N_SEMS,)),
            pltpu.SemaphoreType.DMA((N_SEMS,)),
            pltpu.SemaphoreType.DMA((9,)),
        ],
        compiler_params=pltpu.CompilerParams(
            collective_id=0, has_side_effects=True, vmem_limit_bytes=40 * 2**20
        ),
        cost_estimate=pl.CostEstimate(flops=4 * 10**9, bytes_accessed=150 * 10**6, transcendentals=0),
    )(
        slot_seq.T,
        neighbour_count,
        neighbour_embed,
        cond_keys.T,
        cond_values.T,
        enc_query.T.reshape(2, 96, 768),
        enc_out.reshape(2, 96, 768),
        key_weight_matrix,
        value_weight_matrix,
        queries,
        neighbour_ids,
        enc_gain.reshape(1, 768),
        final_gain.reshape(1, 768),
    )
    mixed_out = jnp.dot(attended, out_rows, preferred_element_type=jnp.float32)
    return (hidden.astype(jnp.float32) + mixed_out).astype(jnp.bfloat16)


def solution(mesh):
    in_specs = (
        P(("ctx", "nbr"), "tp"),
        P(("ctx", "nbr"), "tp"),
        P("ctx", "tp"),
        P("ctx", "tp"),
        P("ctx", "tp"),
        P(("ctx", "nbr"), None, None),
        P(("ctx", "nbr"), None),
        P(("ctx", "nbr")),
        P(),
        P(("ctx", "nbr"), "tp"),
        P(("ctx", "nbr"), "tp"),
        P(),
        P(None, "tp"),
        P("tp", None),
        P(),
    )
    out_specs = P(("ctx", "nbr"), "tp")
    return jax.shard_map(
        per_device, mesh=mesh, in_specs=in_specs, out_specs=out_specs, check_vma=False
    )
```

time: 220 us -> 110 us (0.50)
  waiting for transfers between devices: 82.3 us -> 0.73 us
  Pallas kernels: 0 us -> 78.6 us
  blocking collectives: 59.2 us -> 0 us
  starting transfers between devices: 18.7 us -> 0.01 us
  matrix products: 17.6 us -> 4.23 us
  other arithmetic: 10.8 us -> 0 us
  local copies, waits for them, and re-layouts: 17 us -> 11.1 us
    pallas_call x0 -> x1, Pallas kernels: none -> 78.6 us  [per_device(): pl.pallas_call(body, out_shape=jax.ShapeDtypeStruct((256, 2048), bf16), i...]
    all_gather x2 -> x0, blocking collectives: 40.6 us -> none  [the longest x1 23.3 us: per_device(): lax.all_gather(key_weight_matrix, 'ctx', axis=0, tiled=True)]
    all_gather x3 -> x1, waiting for transfers between devices: 32.3 us -> 0.02 us  [per_device(): out_rows = lax.all_gather(w_out, 'ctx', axis=0, tiled=True)]
    reduce_scatter x1 -> x0, waiting for transfers between devices: 27.2 us -> none  [per_device(): lax.psum_scatter(term.astype(jnp.bfloat16), 'tp', scatter_dimension=0, ti...]
    all_to_all x1 -> x0, blocking collectives: 18.6 us -> none  [per_device(): lax.all_to_all(encoded.reshape(owners, per_owner, quarter, enc_width), 'n...]
    all_to_all x2 -> x0, waiting for transfers between devices: 16.1 us -> none  [the longest x1 8.67 us: per_device(): lax.all_to_all(sent_keys, 'nbr', split_axis=0, concat_axis=0, tiled=True)]
    all_to_all x2 -> x0, starting transfers between devices: 14.3 us -> none  [the longest x1 10.9 us: per_device(): lax.all_to_all(sent_keys, 'nbr', split_axis=0, concat_axis=0, tiled=True)]
    dot_general x10 -> x1, matrix products: 17.2 us -> 4.23 us  [per_device(): mixed_out = jnp.dot(attended, out_rows, preferred_element_type=jnp.float32)]
  transfers between devices with their start and end apart: 8 -> 1, of which waited for: 6 -> 0; matrix products, arithmetic and copies ran while one was open for 12% -> 1% of each run, Pallas kernels for 0% -> 73%
where the time goes in v1:
time: 110 us; the launch traced here: 108 us
  Pallas kernels  78.6 us (71%)
  between operations  13.4 us (12%)
  local copies, waits for them, and re-layouts  11.1 us (10%)
  matrix products  4.23 us (4%)
    pallas_call x1, Pallas kernels, per_device(): pl.pallas_call(body, out_shape=jax.ShapeDtypeStruct((256, 2048), bf16), i...  78.6 us
    unnamed x24, local copies, waits for them, and re-layouts  9.69 us
    dot_general x1, matrix products, per_device(): mixed_out = jnp.dot(attended, out_rows, preferred_element_type=jnp.float32)  4.23 us
  transfers between devices with their start and end apart: 1, of which 0 were waited for; matrix products, arithmetic and copies ran while one was open for 1% of the time, Pallas kernels for 73%

profile of v1, /device:TPU:1, one launch (start us, length us, event | category | flops | bytes accessed | tf_op | source)
XLA Modules:
  0.0 108.0 jit_solution(10700728449102140330)
XLA Ops:
  6.5 0.0 all-gather.2.cloned.1.call-start
  6.5 0.7 all-gather.2.cloned.1.call-update
  7.3 0.7 reshape.14.gain_in
  7.9 0.7 reshape.15.gain_out
  8.6 0.0 copy-start
  8.6 1.4 %copy-done = bf16[8,128,768]{2,1,0:T(8,128)(2,1)S(1)} copy-done((bf16[8,128,768]{2,1,0:T(8,128)(2,1)S(1)}, bf16[8,128,768]{2,1,0:T(8,128)(2,1)}, u32[]{:S(2)}) %copy-start) | copy-done | bytes 1572888
  10.0 0.0 copy-start.1
  10.0 1.0 copy-done.1
  11.0 0.0 copy-start.2
  11.0 1.0 copy-done.2
  12.0 0.0 copy-start.3
  12.0 0.9 copy-done.3
  12.9 0.0 copy-start.4
  12.9 0.9 copy-done.4
  13.8 0.0 copy-start.5
  13.8 0.9 copy-done.5
  14.7 0.0 copy-start.6
  14.7 0.8 copy-done.6
  15.5 0.0 copy-start.7
  15.5 0.8 copy-done.7
  16.3 0.0 copy-start.8
  16.3 0.7 copy-done.8
  17.0 0.0 copy-start.9
  17.0 0.7 copy-done.9
  17.7 0.0 copy-start.10
  17.7 0.7 copy-done.10
  18.3 0.0 copy-start.11
  18.3 78.6 %shard_map.145 = bf16[256,2048]{1,0:T(8,128)(2,1)S(1)} custom-call(s32[8,128]{1,0:T(8,128)S(1)} %bitcast.13, s32[4]{0:T(128)S(1)} %copy-done.10, bf16[8,128,768]{2,1,0:T(8,128)(2,1)S(1)} %copy-done, bf16[192,256]{1,0:T(8,128)(2,1)S(1)} %bitcast.11, bf16[192,256]{1,0:T(8,128)(2,1)S(1)} %bitcast.12, bf16[2,96,768]{2,1,0:T(8,128)(2,1)S(1)} %bitcast.9, ...), custom_call_target="tpu_custom_call" | custom-call | flops 4000000000 | bytes 150000000 | tf_op jit(solution)/shard_map/pallas_call | solution.py:371
  96.9 0.0 all-gather.2.cloned.1.call-done
  96.9 0.0 copy-done.11
  96.9 4.2 %fusion = bf16[256,1024]{1,0:T(8,128)(2,1)} fusion(bf16[256,2048]{1,0:T(8,128)(2,1)S(1)} %shard_map.145, bf16[2048,1024]{1,0:T(8,128)(2,1)} %all-gather.2.cloned.1.call-done, bf16[256,1024]{1,0:T(8,128)(2,1)S(1)} %copy-done.11), kind=kOutput, calls=%fused_computation.1 | convolution fusion | flops 1074528256 | bytes 6291456 | tf_op jit(solution)/shard_map/dot_general | solution.py:421
Async XLA Ops:
  6.5 90.4 %all-gather.2.cloned.1.call-start = ((), (), s32[]{:S(2)}) async-start(), calls=%async_computation | async-start | bytes 4456448 | tf_op jit(solution)/shard_map/all_gather | solution.py:367
  8.6 1.4 %copy-start = (bf16[8,128,768]{2,1,0:T(8,128)(2,1)S(1)}, bf16[8,128,768]{2,1,0:T(8,128)(2,1)}, u32[]{:S(2)}) copy-start(bf16[8,128,768]{2,1,0:T(8,128)(2,1)} %embed.1) | copy-start | bytes 4718596
  10.0 1.0 copy-start.1
  11.0 1.0 copy-start.2
  12.0 0.9 copy-start.3
  12.9 0.9 copy-start.4
  13.8 0.9 copy-start.5
  14.7 0.8 copy-start.6
  15.5 0.8 copy-start.7
  16.3 0.7 copy-start.8
  17.0 0.7 copy-start.9
  17.7 0.7 copy-start.10
  18.3 78.6 %copy-start.11 = (bf16[256,1024]{1,0:T(8,128)(2,1)S(1)}, bf16[256,1024]{1,0:T(8,128)(2,1)}, u32[]{:S(2)}) copy-start(bf16[256,1024]{1,0:T(8,128)(2,1)} %param.15) | copy-start | bytes 1572868
Sparse Core Ops, SparseCore 0:
  9.5 54.0 all-gather.1

commit v2 on v1

--- a/solution.py
+++ b/solution.py
@@ -15,10 +15,11 @@
 TN = (((0,), (0,)), ((), ()))
 NN = (((1,), (0,)), ((), ()))
 
-S_EMB, S_COND, S_ENC_W, S_KV_RIGHT, S_KV_LEFT, S_KV_MATE, S_MASK, S_AG, S_PREV, S_ATT = (
+S_EMB, S_COND, S_ENC_W, S_KV_RIGHT, S_KV_LEFT, S_KV_MATE, S_QUERY, S_AG, S_PREV, S_ATT = (
     0, 2, 5, 13, 17, 20, 21, 22, 28, 29,
 )
-N_SEMS = 35
+S_OUT_RIGHT, S_OUT_LEFT, S_OUT_MATE = 35, 39, 42
+N_SEMS = 50
 
 
 def dot(a, b, dims):
@@ -31,11 +32,11 @@
 
 
 def body(
-    slots, counts, embed, cond_k_far, cond_v_far, enc_q, enc_o, key_w, value_w, queries_far, ids_far, gain_in, gain_out,
-    attended,
-    cond_k, cond_v, queries, ids,
-    emb, packs, cond_send, cond, enc_w, normed, mixed, encoded, kv_w, keys, values,
-    last_send, last_got, mask_send, mask_got, key_mask, partial, send, recv, local,
+    slots, counts, embed, cond_k_far, cond_v_far, enc_q, enc_o, key_w, value_w, queries_far, ids_far, w_far, hidden_far,
+    gain_in, gain_out,
+    output,
+    cond_k, cond_v, queries, ids, w_out, hidden, total, attended, queries_next, rows_send, rows_got,
+    emb, packs, cond_send, cond, enc_w, normed, mixed, encoded, kv_w, keys, values, key_mask, send, recv, local,
 ):
     c, n, t = lax.axis_index("ctx"), lax.axis_index("nbr"), lax.axis_index("tp")
     block = c * 8 + n
@@ -75,6 +76,8 @@
         pltpu.make_async_copy(cond_v_far, cond_v, local.at[6]),
         pltpu.make_async_copy(queries_far, queries, local.at[7]),
         pltpu.make_async_copy(ids_far, ids, local.at[8]),
+        pltpu.make_async_copy(w_far, w_out.at[y, core], local.at[9]),
+        pltpu.make_async_copy(hidden_far, hidden, local.at[10]),
     ]
     for made in own:
         made.start()
@@ -82,6 +85,7 @@
     barrier = pltpu.get_barrier_semaphore()
     for device in (
         (c, n, right), (c, n, left), (c, n, across), (mate, n, t), (c_right, n, t), (c_left, n, t), before_device,
+        next_device,
     ):
         pl.semaphore_signal(barrier, inc=1, device_id=device, device_id_type=MESH)
     for k in range(2):
@@ -92,7 +96,7 @@
             pl.semaphore_signal(barrier, inc=1, device_id=(c, other, t), device_id_type=MESH)
 
     with_self = jnp.where(lax.rem(2 * n, 4) == t, 1, 0)
-    pl.semaphore_wait(barrier, 9 - with_self)
+    pl.semaphore_wait(barrier, 10 - with_self)
 
     mine = n // 4
 
@@ -115,6 +119,38 @@
     own[1].wait()
     to(enc_w.at[:, t, core], S_ENC_W, (c, n, right))
     to(enc_w.at[:, t, core], S_ENC_W + 1, (c, n, left))
+
+    own[2].wait()
+    own[3].wait()
+
+    def kv_right(s):
+        to(kv_w.at[:, lax.rem(y - s + 8, 8), core], S_KV_RIGHT + s, (c_right, n, t))
+
+    def kv_left(s):
+        to(kv_w.at[:, lax.rem(y + s, 8), core], S_KV_LEFT + s, (c_left, n, t))
+
+    def kv_right_in(s):
+        arrived(kv_w.at[:, lax.rem(y - s - 1 + 8, 8), core], S_KV_RIGHT + s)
+
+    def kv_left_in(s):
+        arrived(kv_w.at[:, lax.rem(y + s + 1, 8), core], S_KV_LEFT + s)
+
+    def out_right(s):
+        to(w_out.at[lax.rem(y - s + 8, 8), core], S_OUT_RIGHT + s, (c_right, n, t))
+
+    def out_left(s):
+        to(w_out.at[lax.rem(y + s, 8), core], S_OUT_LEFT + s, (c_left, n, t))
+
+    def out_right_in(s):
+        arrived(w_out.at[lax.rem(y - s - 1 + 8, 8), core], S_OUT_RIGHT + s)
+        to(w_out.at[lax.rem(y - s - 1 + 8, 8), core], S_OUT_MATE + 1 + s, (mate, n, t))
+
+    def out_left_in(s):
+        arrived(w_out.at[lax.rem(y + s + 1, 8), core], S_OUT_LEFT + s)
+        to(w_out.at[lax.rem(y + s + 1, 8), core], S_OUT_MATE + 5 + s, (mate, n, t))
+
+    kv_right(0)
+    kv_left(0)
 
     own[4].wait()
     own[5].wait()
@@ -130,35 +166,37 @@
     for k in range(2):
         cond[t, k] = packs[slots[first + 4 * k, block] // 2]
 
-    own[2].wait()
-    own[3].wait()
-
-    def kv_right(s):
-        to(kv_w.at[:, lax.rem(y - s + 8, 8), core], S_KV_RIGHT + s, (c_right, n, t))
-
-    def kv_left(s):
-        to(kv_w.at[:, lax.rem(y + s, 8), core], S_KV_LEFT + s, (c_left, n, t))
-
-    def kv_right_in(s):
-        arrived(kv_w.at[:, lax.rem(y - s - 1 + 8, 8), core], S_KV_RIGHT + s)
-
-    def kv_left_in(s):
-        arrived(kv_w.at[:, lax.rem(y + s + 1, 8), core], S_KV_LEFT + s)
-
-    kv_right(0)
-    kv_left(0)
+    own[6].wait()
+    to(queries.at[pl.ds(0, STRETCH_TOKENS)], S_QUERY, before_device, dst=queries_next)
+    own[8].wait()
+    out_right(0)
+    out_left(0)
+    to(w_out.at[y, core], S_OUT_MATE, (mate, n, t))
 
     own[7].wait()
     row = lax.broadcasted_iota(jnp.int32, (8, 128), 0)
     count = jnp.zeros((8, 128), jnp.int32)
     for st in range(4):
         count = jnp.where(row // 2 == st, counts[st], count)
-    mask_send[...] = jnp.where((lax.rem(row, 2) < count) & (ids[...] != 0), 1.0, 0.0)
-    to(mask_send, S_MASK, next_device, dst=mask_got)
-    mask = mask_send[...]
+    mask = jnp.where((lax.rem(row, 2) < count) & (ids[...] != 0), 1.0, 0.0)
     for s in range(8):
         key_mask[s] = jnp.broadcast_to(mask[s : s + 1], (128, 128)).T
 
+    kv_right_in(0)
+    kv_right(1)
+    kv_left_in(0)
+    kv_left(1)
+    arrived(enc_w.at[:, left, core], S_ENC_W)
+    to(enc_w.at[0, left, core], S_ENC_W + 2, (c, n, right))
+    to(enc_w.at[:, left, core], S_ENC_W + 4, (mate, n, t))
+    arrived(enc_w.at[:, right, core], S_ENC_W + 1)
+    to(enc_w.at[1, right, core], S_ENC_W + 3, (c, n, left))
+    to(enc_w.at[:, right, core], S_ENC_W + 5, (mate, n, t))
+    kv_right_in(1)
+    kv_right(2)
+    kv_left_in(1)
+    kv_left(2)
+
     for k in range(2):
         other = first + 4 * k
 
@@ -170,7 +208,7 @@
         def _():
             pltpu.make_async_copy(embed.at[n], emb.at[k], local.at[4]).wait()
 
-        normed[k] = norm_rows(emb[k].astype(jnp.float32), gain_in[...].astype(jnp.float32))
+        normed[k] = norm_rows(emb[k].astype(jnp.float32), gain_in[...].astype(jnp.float32).reshape(1, 768))
 
     def encode_heads(shard):
         query = dot(enc_w[0, shard].reshape(192, 768), normed[...].reshape(256, 768), NT)
@@ -190,41 +228,30 @@
         mixed[shard] = jnp.concatenate(columns, axis=1)
 
     encode_heads(t)
-
-    kv_right_in(0)
-    kv_right(1)
-    kv_left_in(0)
-    kv_left(1)
-
-    arrived(enc_w.at[:, left, core], S_ENC_W)
-    to(enc_w.at[0, left, core], S_ENC_W + 2, (c, n, right))
-    to(enc_w.at[:, left, core], S_ENC_W + 4, (mate, n, t))
-    arrived(enc_w.at[:, right, core], S_ENC_W + 1)
-    to(enc_w.at[1, right, core], S_ENC_W + 3, (c, n, left))
-    to(enc_w.at[:, right, core], S_ENC_W + 5, (mate, n, t))
-    arrived(cond.at[left], S_COND)
-    arrived(enc_w.at[:, left, 1 - core], S_ENC_W + 4)
-    encode_heads(left)
-    kv_right_in(1)
-    kv_right(2)
-    kv_left_in(1)
-    kv_left(2)
     arrived(enc_w.at[0, across, core], S_ENC_W + 2)
     to(enc_w.at[0, across, core], S_ENC_W + 6, (mate, n, t))
     arrived(enc_w.at[1, across, core], S_ENC_W + 3)
     to(enc_w.at[1, across, core], S_ENC_W + 7, (mate, n, t))
+    out_right_in(0)
+    out_right(1)
+    out_left_in(0)
+    out_left(1)
+    arrived(cond.at[left], S_COND)
+    arrived(enc_w.at[:, left, 1 - core], S_ENC_W + 4)
+    encode_heads(left)
+    kv_right_in(2)
+    kv_right(3)
+    kv_left_in(2)
     arrived(cond.at[right], S_COND + 2)
     arrived(enc_w.at[:, right, 1 - core], S_ENC_W + 5)
     encode_heads(right)
-    kv_right_in(2)
-    kv_right(3)
     arrived(cond.at[across], S_COND + 1)
     arrived(enc_w.at[0, across, 1 - core], S_ENC_W + 6)
     encode_heads(across)
     arrived(enc_w.at[1, across, 1 - core], S_ENC_W + 7)
 
     updated = dot(mixed[...].reshape(768, 256), enc_w[1].reshape(768, 768), TN)
-    gain = gain_out[...].astype(jnp.float32)
+    gain = gain_out[...].astype(jnp.float32).reshape(1, 768)
     for k in range(2):
         rows = emb[k].astype(jnp.float32) + updated[k * 128 : (k + 1) * 128]
         encoded[first + 4 * k] = norm_rows(rows, gain)
@@ -233,9 +260,12 @@
         to(encoded.at[first + 4 * k], S_AG + 2 * k, (c, n, right))
         to(encoded.at[first + 4 * k], S_AG + 2 * k + 1, (c, n, left))
 
-    kv_left_in(2)
     kv_right_in(3)
     to(kv_w.at[:, :, core], S_KV_MATE, (mate, n, t))
+    out_right_in(1)
+    out_right(2)
+    out_left_in(1)
+    out_left(2)
     arrived(kv_w.at[:, :, 1 - core], S_KV_MATE)
 
     def project(rows):
@@ -263,8 +293,13 @@
     project_pair(first_of(left))
     arrived(encoded.at[first_of(right)], S_AG + 1)
     project_pair(first_of(right))
+    out_right_in(2)
+    out_right(3)
+    out_left_in(2)
     arrived(encoded.at[first_of(across)], S_AG + 4)
     arrived(encoded.at[first_of(across) + 4], S_AG + 5)
+
+    project_pair(first_of(across))
 
     slot_of = []
     for s in range(8):
@@ -272,70 +307,77 @@
         for o in range(1, 8):
             place = jnp.where(slots[o, block] == s, o, place)
         slot_of.append(place)
-    for k in range(2):
-        last_send[k] = encoded[slot_of[6 + k]]
-    to(last_send, S_PREV, next_device, dst=last_got)
-    project_pair(first_of(across))
-
-    own[6].wait()
+
     lane = lax.broadcasted_iota(jnp.int32, (1, 128), 1)
-
-    def attend(key_rows, value_rows, allowed, h, start, low, high):
-        at = slice(h * HEAD_WIDTH, (h + 1) * HEAD_WIDTH)
-        scores = dot(key_rows, queries[start : start + 128, at], NT) * HEAD_WIDTH ** (-0.5)
-        scores = jnp.where(allowed > 0, scores, -1e30)
-        raised = jnp.exp(scores - jnp.max(scores, axis=0, keepdims=True)) * allowed
-        total = jnp.sum(raised, axis=0, keepdims=True)
-        use = (total > 0) & (lane >= low) & (lane < high)
-        share = jnp.where(use, 1.0 / jnp.where(use, total, 1.0), 0.0)
-        return dot((raised * share).astype(jnp.bfloat16), value_rows, TN)
-
-    def stretch_attend(st, h, start, low, high):
+    use_lane = (lane >= STRETCH_TOKENS - 1) & (lane < 2 * STRETCH_TOKENS - 1)
+
+    def attend(st, h, query_rows):
         at = slice(h * HEAD_WIDTH, (h + 1) * HEAD_WIDTH)
         pair = (slot_of[2 * st], slot_of[2 * st + 1])
         key_rows = jnp.concatenate([keys[p, :, at] for p in pair], axis=0)
         value_rows = jnp.concatenate([values[p, :, at] for p in pair], axis=0)
         allowed = key_mask[2 * st : 2 * st + 2].reshape(256, 128)
-        return attend(key_rows, value_rows, allowed, h, start, low, high)
-
-    for h in range(4):
-        at = slice(h * HEAD_WIDTH, (h + 1) * HEAD_WIDTH)
-        one = stretch_attend(0, h, 0, 63, 127)
-        two = stretch_attend(1, h, 64, 63, 127)
-        three = stretch_attend(2, h, 128, 63, 127)
-        four = stretch_attend(3, h, 128, 127, 128)
-        partial[:, at] = jnp.concatenate([one[:64], one[64:] + two[:64]], axis=0)
-        lower = jnp.concatenate([two[64:] + three[:64] + four[:64], three[64:] + four[64:]], axis=0)
-        attended[128:256, pl.ds(pl.multiple_of(t * 512 + h * 128, 128), 128)] = lower.astype(jnp.bfloat16)
+        scores = dot(key_rows, query_rows, NT) * HEAD_WIDTH ** (-0.5)
+        scores = jnp.where(allowed > 0, scores, -1e30)
+        raised = jnp.exp(scores - jnp.max(scores, axis=0, keepdims=True)) * allowed
+        sums = jnp.sum(raised, axis=0, keepdims=True)
+        use = (sums > 0) & use_lane
+        share = jnp.where(use, 1.0 / jnp.where(use, sums, 1.0), 0.0)
+        return dot((raised * share).astype(jnp.bfloat16), value_rows, TN)
+
+    heads = [slice(h * HEAD_WIDTH, (h + 1) * HEAD_WIDTH) for h in range(4)]
+    arrived(queries_next, S_QUERY)
+    fourth = []
+    for h, at in enumerate(heads):
+        got = attend(3, h, jnp.concatenate([queries[192:256, at], queries_next[:, at]], axis=0))
+        rows_send[:, at] = got[64:].astype(jnp.bfloat16)
+        fourth.append(got[:64])
+    to(rows_send, S_PREV, next_device, dst=rows_got)
+
+    second = []
+    for h, at in enumerate(heads):
+        three = attend(2, h, queries[128:256, at])
+        two = attend(1, h, queries[64:192, at])
+        lower = jnp.concatenate([two[64:] + three[:64], three[64:] + fourth[h]], axis=0)
+        attended[t, 128:256, at] = lower.astype(jnp.bfloat16)
+        second.append(two[:64])
 
     def piece(half, shard):
-        return attended.at[pl.ds(128 * half, 128), pl.ds(pl.multiple_of(shard * 512, 512), 512)]
+        return attended.at[shard, pl.ds(128 * half, 128)]
 
     to(piece(1, t), S_ATT, (c, n, right))
     to(piece(1, t), S_ATT + 1, (c, n, left))
 
-    arrived(mask_got, S_MASK)
-    seen = mask_got[...] * jnp.where(block > 0, 1.0, 0.0)
-    allowed = jnp.concatenate(
-        [jnp.broadcast_to(seen[6 + k : 7 + k], (128, 128)).T for k in range(2)], axis=0
-    )
-    arrived(last_got, S_PREV)
-    got_k, got_v = project(last_got[...].reshape(256, 768))
-    for h in range(4):
-        at = slice(h * HEAD_WIDTH, (h + 1) * HEAD_WIDTH)
-        upper = partial[:, at] + attend(got_k[:, at], got_v[:, at], allowed, h, 0, 0, 63)
-        attended[0:128, pl.ds(pl.multiple_of(t * 512 + h * 128, 128), 128)] = upper.astype(jnp.bfloat16)
-
+    ones = [attend(0, h, queries[0:128, at]) for h, at in enumerate(heads)]
+    arrived(rows_got, S_PREV)
+    for h, at in enumerate(heads):
+        before_rows = jnp.where(block > 0, rows_got[:, at].astype(jnp.float32), 0.0)
+        upper = jnp.concatenate([ones[h][:64] + before_rows, ones[h][64:] + second[h]], axis=0)
+        attended[t, 0:128, at] = upper.astype(jnp.bfloat16)
     to(piece(0, t), S_ATT + 2, (c, n, right))
     to(piece(0, t), S_ATT + 3, (c, n, left))
+
+    out_right_in(3)
+    for i in range(8):
+        at = y if i == 0 else (y - i + 8 if i < 5 else y + i - 4)
+        arrived(w_out.at[lax.rem(at, 8), 1 - core], S_OUT_MATE + i)
+    own[9].wait()
+
+    def product(shard):
+        return dot(attended[shard], w_out[pl.ds(2 * shard, 2)].reshape(512, 1024), NN)
+
     arrived(piece(1, left), S_ATT)
     to(piece(1, left), S_ATT + 4, (c, n, right))
+    total[...] = hidden[...].astype(jnp.float32) + product(t)
     arrived(piece(0, right), S_ATT + 3)
     to(piece(0, right), S_ATT + 5, (c, n, left))
+    arrived(piece(0, left), S_ATT + 2)
+    total[...] += product(left)
     arrived(piece(1, right), S_ATT + 1)
-    arrived(piece(0, left), S_ATT + 2)
+    total[...] += product(right)
     arrived(piece(1, across), S_ATT + 4)
     arrived(piece(0, across), S_ATT + 5)
+    output[...] = (total[...] + product(across)).astype(jnp.bfloat16)
 
     for k in range(2):
 
@@ -364,20 +406,26 @@
     enc_out,
     final_gain,
 ):
-    out_rows = lax.all_gather(w_out, "ctx", axis=0, tiled=True)
     vmem, hbm = pl.BlockSpec(memory_space=pltpu.VMEM), pl.BlockSpec(memory_space=pltpu.HBM)
     smem = pl.BlockSpec(memory_space=pltpu.SMEM)
     bf16, f32 = jnp.bfloat16, jnp.float32
-    attended = pl.pallas_call(
+    return pl.pallas_call(
         body,
-        out_shape=jax.ShapeDtypeStruct((256, 2048), bf16),
-        in_specs=[smem, smem, *[hbm] * 9, vmem, vmem],
+        out_shape=jax.ShapeDtypeStruct((256, 1024), bf16),
+        in_specs=[smem, smem, *[hbm] * 11, vmem, vmem],
         out_specs=vmem,
         scratch_shapes=[
             pltpu.VMEM((192, 256), bf16),
             pltpu.VMEM((192, 256), bf16),
             pltpu.VMEM((256, 512), bf16),
             pltpu.VMEM((8, 128), jnp.int32),
+            pltpu.VMEM((8, 2, 128, 1024), bf16),
+            pltpu.VMEM((256, 1024), bf16),
+            pltpu.VMEM((256, 1024), f32),
+            pltpu.VMEM((4, 256, 512), bf16),
+            pltpu.VMEM((64, 512), bf16),
+            pltpu.VMEM((64, 512), bf16),
+            pltpu.VMEM((64, 512), bf16),
             pltpu.VMEM((2, 128, 768), bf16),
             pltpu.VMEM((4, 192, 128), bf16),
             pltpu.VMEM((3, 2, 192, 128), bf16),
@@ -389,18 +437,13 @@
             pltpu.VMEM((2, 8, 2, 48, 512), bf16),
             pltpu.VMEM((8, 128, 512), bf16),
             pltpu.VMEM((8, 128, 512), bf16),
-            pltpu.VMEM((2, 128, 768), bf16),
-            pltpu.VMEM((2, 128, 768), bf16),
-            pltpu.VMEM((8, 128), f32),
-            pltpu.VMEM((8, 128), f32),
             pltpu.VMEM((8, 128, 128), f32),
-            pltpu.VMEM((128, 512), f32),
             pltpu.SemaphoreType.DMA((N_SEMS,)),
             pltpu.SemaphoreType.DMA((N_SEMS,)),
-            pltpu.SemaphoreType.DMA((9,)),
+            pltpu.SemaphoreType.DMA((11,)),
         ],
         compiler_params=pltpu.CompilerParams(
-            collective_id=0, has_side_effects=True, vmem_limit_bytes=40 * 2**20
+            collective_id=0, has_side_effects=True, vmem_limit_bytes=62 * 2**20
         ),
         cost_estimate=pl.CostEstimate(flops=4 * 10**9, bytes_accessed=150 * 10**6, transcendentals=0),
     )(
@@ -415,11 +458,11 @@
         value_weight_matrix,
         queries,
         neighbour_ids,
-        enc_gain.reshape(1, 768),
-        final_gain.reshape(1, 768),
+        w_out,
+        hidden,
+        enc_gain,
+        final_gain,
     )
-    mixed_out = jnp.dot(attended, out_rows, preferred_element_type=jnp.float32)
-    return (hidden.astype(jnp.float32) + mixed_out).astype(jnp.bfloat16)
 
 
 def solution(mesh):

time: 110 us -> 69 us (0.63); the launches traced: 108 us -> 68.8 us
  between operations: 13.4 us -> 0.01 us
  Pallas kernels: 78.6 us -> 66.9 us
  local copies, waits for them, and re-layouts: 11.1 us -> 1.87 us
  matrix products: 4.23 us -> 0 us
    pallas_call x1, Pallas kernels: 78.6 us -> 66.9 us  [per_device(): pl.pallas_call(body, out_shape=jax.ShapeDtypeStruct((256, 1024), bf16), i...]
    unnamed x24 -> x1, local copies, waits for them, and re-layouts: 9.69 us -> 1.87 us
    dot_general x1 -> x0, matrix products: 4.23 us -> none  [per_device(): mixed_out = jnp.dot(attended, out_rows, preferred_element_type=jnp.float32)]
    reshape x2 -> x0, local copies, waits for them, and re-layouts: 1.37 us -> none  [the longest x1 0.69 us: per_device(): enc_gain.reshape(1, 768)]
  transfers between devices with their start and end apart: 1 -> 0, of which waited for: 0 -> 0; matrix products, arithmetic and copies ran while one was open for 1% -> 0% of each run, Pallas kernels for 73% -> 0%
where the time goes in v2:
time: 69 us; the launch traced here: 68.8 us
  Pallas kernels  66.9 us (97%)
  local copies, waits for them, and re-layouts  1.87 us (3%)
    pallas_call x1, Pallas kernels, per_device(): pl.pallas_call(body, out_shape=jax.ShapeDtypeStruct((256, 1024), bf16), i...  66.9 us
    unnamed x1, local copies, waits for them, and re-layouts  1.87 us

profile of v2, /device:TPU:1, one launch (start us, length us, event | category | flops | bytes accessed | tf_op | source)
XLA Modules:
  0.0 68.8 jit_solution(4979665583748016473)
XLA Ops:
  0.0 66.9 %shard_map.145 = bf16[256,1024]{1,0:T(8,128)(2,1)} custom-call(s32[8,128]{1,0:T(8,128)} %bitcast.11, s32[4]{0:T(128)} %counts.1, bf16[8,128,768]{2,1,0:T(8,128)(2,1)} %embed.1, bf16[192,256]{1,0:T(8,128)(2,1)} %bitcast.9, bf16[192,256]{1,0:T(8,128)(2,1)} %bitcast.10, bf16[2,96,768]{2,1,0:T(8,128)(2,1)} %bitcast.7, bf16[2,96,768]{2,1,0:T(8,128)(2,1)} %bitcast.8, ...), custom_call_target="tpu_custom_call" | custom-call | flops 4000000000 | bytes 150000000 | tf_op jit(solution)/shard_map/pallas_call | solution.py:412
  66.9 1.9 %copy.17 = bf16[256,1024]{1,0:T(8,128)(2,1)} copy(bf16[256,1024]{1,0:T(8,128)(2,1)} %shard_map.145) | data formatting | bytes 1048576

commit v3 on v2

--- a/solution.py
+++ b/solution.py
@@ -15,11 +15,11 @@
 TN = (((0,), (0,)), ((), ()))
 NN = (((1,), (0,)), ((), ()))
 
-S_EMB, S_COND, S_ENC_W, S_KV_RIGHT, S_KV_LEFT, S_KV_MATE, S_QUERY, S_AG, S_PREV, S_ATT = (
-    0, 2, 5, 13, 17, 20, 21, 22, 28, 29,
+S_EMB, S_COND, S_ENC_Q, S_ENC_O, S_KV_RIGHT, S_KV_LEFT, S_KV_MATE, S_QUERY, S_AG, S_PREV = (
+    0, 2, 6, 14, 22, 26, 29, 30, 31, 37,
 )
-S_OUT_RIGHT, S_OUT_LEFT, S_OUT_MATE = 35, 39, 42
-N_SEMS = 50
+S_OUT_RIGHT, S_OUT_LEFT, S_OUT_MATE, S_ATT = 38, 42, 45, 53
+N_SEMS = 65
 
 
 def dot(a, b, dims):
@@ -36,7 +36,7 @@
     gain_in, gain_out,
     output,
     cond_k, cond_v, queries, ids, w_out, hidden, total, attended, queries_next, rows_send, rows_got,
-    emb, packs, cond_send, cond, enc_w, normed, mixed, encoded, kv_w, keys, values, key_mask, send, recv, local,
+    emb, packs, cond_send, cond_own, cond_side, cond_across, enc_w, normed, mixed, encoded, kv_w, keys, values, key_mask, send, recv, local,
 ):
     c, n, t = lax.axis_index("ctx"), lax.axis_index("nbr"), lax.axis_index("tp")
     block = c * 8 + n
@@ -115,10 +115,38 @@
         def _():
             pltpu.make_async_copy(embed.at[n], emb.at[mine], local.at[4]).start()
 
-    own[0].wait()
-    own[1].wait()
-    to(enc_w.at[:, t, core], S_ENC_W, (c, n, right))
-    to(enc_w.at[:, t, core], S_ENC_W + 1, (c, n, left))
+    def enc_half(i, shard, of=None, part=None):
+        rows = enc_w.at[i, shard, core if of is None else of]
+        return rows if part is None else rows.at[pl.ds(48 * part, 48)]
+
+    enc_sem = (S_ENC_Q, S_ENC_O)
+
+    def enc_send(i):
+        source = (enc_q, enc_o)[i].at[core]
+        to(source, enc_sem[i], (c, n, right), dst=enc_half(i, t))
+        to(source, enc_sem[i] + 1, (c, n, left), dst=enc_half(i, t))
+
+    def enc_pass_on(i):
+        arrived(enc_half(i, left), enc_sem[i])
+        to(enc_half(i, left, part=0), enc_sem[i] + 2, (c, n, right))
+        to(enc_half(i, left), enc_sem[i] + 4, (mate, n, t))
+        arrived(enc_half(i, right), enc_sem[i] + 1)
+        to(enc_half(i, right, part=1), enc_sem[i] + 3, (c, n, left))
+        to(enc_half(i, right), enc_sem[i] + 5, (mate, n, t))
+
+    def enc_last(i):
+        for part in range(2):
+            arrived(enc_half(i, across, part=part), enc_sem[i] + 2 + part)
+            to(enc_half(i, across, part=part), enc_sem[i] + 6 + part, (mate, n, t))
+
+    def enc_mate(i, shard, at):
+        arrived(enc_half(i, shard, 1 - core), enc_sem[i] + at)
+
+    def enc_mate_across(i):
+        for part in range(2):
+            arrived(enc_half(i, across, 1 - core, part), enc_sem[i] + 6 + part)
+
+    enc_send(0)
 
     own[2].wait()
     own[3].wait()
@@ -157,14 +185,16 @@
     for st in range(4):
         at = slice(st * STRETCH_TOKENS, (st + 1) * STRETCH_TOKENS)
         packs[st] = jnp.concatenate([cond_k[:, at], cond_v[:, at]], axis=1)
-    for d in (1, 3, 2):
-        target = lax.rem(t + d, 4)
-        start = lax.rem(target - n + 8, 4)
+    def pack_for(shard, k):
+        return packs[slots[lax.rem(shard - n + 8, 4) + 4 * k, block] // 2]
+
+    for side, device in enumerate((right, left)):
         for k in range(2):
-            cond_send[d - 1, k] = packs[slots[start + 4 * k, block] // 2]
-        to(cond_send.at[d - 1], S_COND + d - 1, (c, n, target), dst=cond.at[t])
+            cond_send[side, k] = pack_for(device, k)
+        cond_send[side, 2] = pack_for(across, side)
+        to(cond_send.at[side], S_COND + side, (c, n, device), dst=cond_side.at[side])
     for k in range(2):
-        cond[t, k] = packs[slots[first + 4 * k, block] // 2]
+        cond_own[k] = pack_for(t, k)
 
     own[6].wait()
     to(queries.at[pl.ds(0, STRETCH_TOKENS)], S_QUERY, before_device, dst=queries_next)
@@ -186,12 +216,11 @@
     kv_right(1)
     kv_left_in(0)
     kv_left(1)
-    arrived(enc_w.at[:, left, core], S_ENC_W)
-    to(enc_w.at[0, left, core], S_ENC_W + 2, (c, n, right))
-    to(enc_w.at[:, left, core], S_ENC_W + 4, (mate, n, t))
-    arrived(enc_w.at[:, right, core], S_ENC_W + 1)
-    to(enc_w.at[1, right, core], S_ENC_W + 3, (c, n, left))
-    to(enc_w.at[:, right, core], S_ENC_W + 5, (mate, n, t))
+    enc_pass_on(0)
+    enc_send(1)
+    for side, device in enumerate((right, left)):
+        arrived(cond_side.at[side], S_COND + side)
+        to(cond_side.at[side, 2], S_COND + 2 + side, (c, n, device), dst=cond_across.at[side])
     kv_right_in(1)
     kv_right(2)
     kv_left_in(1)
@@ -210,7 +239,11 @@
 
         normed[k] = norm_rows(emb[k].astype(jnp.float32), gain_in[...].astype(jnp.float32).reshape(1, 768))
 
-    def encode_heads(shard):
+    own[0].wait()
+    own[1].wait()
+    enc_last(0)
+
+    def encode_heads(shard, states):
         query = dot(enc_w[0, shard].reshape(192, 768), normed[...].reshape(256, 768), NT)
         query = query.astype(jnp.bfloat16) * jnp.bfloat16(EHD ** (-0.5))
         columns = []
@@ -218,7 +251,7 @@
             rows = []
             for h in range(3):
                 at = slice(h * EHD, (h + 1) * EHD)
-                both = cond[shard, k, at, :]
+                both = states[k, at, :]
                 scores = dot(both, query[at, k * 128 : (k + 1) * 128], TN)[:STRETCH_TOKENS]
                 raised = jnp.exp(scores - jnp.max(scores, axis=0, keepdims=True))
                 weights = (raised / jnp.sum(raised, axis=0, keepdims=True)).astype(jnp.bfloat16)
@@ -227,36 +260,33 @@
             columns.append(jnp.concatenate(rows, axis=0))
         mixed[shard] = jnp.concatenate(columns, axis=1)
 
-    encode_heads(t)
-    arrived(enc_w.at[0, across, core], S_ENC_W + 2)
-    to(enc_w.at[0, across, core], S_ENC_W + 6, (mate, n, t))
-    arrived(enc_w.at[1, across, core], S_ENC_W + 3)
-    to(enc_w.at[1, across, core], S_ENC_W + 7, (mate, n, t))
+    encode_heads(t, cond_own)
+    enc_mate(0, left, 4)
+    encode_heads(left, cond_side.at[0])
+    enc_pass_on(1)
     out_right_in(0)
     out_right(1)
     out_left_in(0)
     out_left(1)
-    arrived(cond.at[left], S_COND)
-    arrived(enc_w.at[:, left, 1 - core], S_ENC_W + 4)
-    encode_heads(left)
+    enc_mate(0, right, 5)
+    encode_heads(right, cond_side.at[1])
     kv_right_in(2)
     kv_right(3)
     kv_left_in(2)
-    arrived(cond.at[right], S_COND + 2)
-    arrived(enc_w.at[:, right, 1 - core], S_ENC_W + 5)
-    encode_heads(right)
-    arrived(cond.at[across], S_COND + 1)
-    arrived(enc_w.at[0, across, 1 - core], S_ENC_W + 6)
-    encode_heads(across)
-    arrived(enc_w.at[1, across, 1 - core], S_ENC_W + 7)
-
-    updated = dot(mixed[...].reshape(768, 256), enc_w[1].reshape(768, 768), TN)
+    for side in range(2):
+        arrived(cond_across.at[side], S_COND + 2 + side)
+    enc_mate_across(0)
+    encode_heads(across, cond_across)
+    enc_last(1)
+    enc_mate(1, left, 4)
+    enc_mate(1, right, 5)
+    enc_mate_across(1)
+
     gain = gain_out[...].astype(jnp.float32).reshape(1, 768)
     for k in range(2):
-        rows = emb[k].astype(jnp.float32) + updated[k * 128 : (k + 1) * 128]
-        encoded[first + 4 * k] = norm_rows(rows, gain)
-
-    for k in range(2):
+        heads_out = mixed[:, :, k * 128 : (k + 1) * 128].reshape(768, 128)
+        updated = dot(heads_out, enc_w[1].reshape(768, 768), TN)
+        encoded[first + 4 * k] = norm_rows(emb[k].astype(jnp.float32) + updated, gain)
         to(encoded.at[first + 4 * k], S_AG + 2 * k, (c, n, right))
         to(encoded.at[first + 4 * k], S_AG + 2 * k + 1, (c, n, left))
 
@@ -334,28 +364,33 @@
         fourth.append(got[:64])
     to(rows_send, S_PREV, next_device, dst=rows_got)
 
-    second = []
-    for h, at in enumerate(heads):
-        three = attend(2, h, queries[128:256, at])
-        two = attend(1, h, queries[64:192, at])
-        lower = jnp.concatenate([two[64:] + three[:64], three[64:] + fourth[h]], axis=0)
-        attended[t, 128:256, at] = lower.astype(jnp.bfloat16)
-        second.append(two[:64])
-
-    def piece(half, shard):
-        return attended.at[shard, pl.ds(128 * half, 128)]
-
-    to(piece(1, t), S_ATT, (c, n, right))
-    to(piece(1, t), S_ATT + 1, (c, n, left))
-
-    ones = [attend(0, h, queries[0:128, at]) for h, at in enumerate(heads)]
+    def piece(i, shard):
+        return attended.at[shard, pl.ds(STRETCH_TOKENS * (3 - i), STRETCH_TOKENS)]
+
+    def leave(i, rows):
+        for h, at in enumerate(heads):
+            attended[t, 64 * (3 - i) : 64 * (4 - i), at] = rows[h].astype(jnp.bfloat16)
+        to(piece(i, t), S_ATT + 3 * i, (c, n, right))
+        to(piece(i, t), S_ATT + 3 * i + 1, (c, n, left))
+
+    def pass_on(i):
+        if i % 2 == 0:
+            arrived(piece(i, left), S_ATT + 3 * i)
+            to(piece(i, left), S_ATT + 3 * i + 2, (c, n, right))
+        else:
+            arrived(piece(i, right), S_ATT + 3 * i + 1)
+            to(piece(i, right), S_ATT + 3 * i + 2, (c, n, left))
+
+    after = fourth
+    for i, st in enumerate((2, 1, 0)):
+        got = [attend(st, h, queries[64 * st : 64 * st + 128, at]) for h, at in enumerate(heads)]
+        leave(i, [got[h][64:] + after[h] for h in range(4)])
+        after = [rows[:64] for rows in got]
+        if i > 0:
+            pass_on(i - 1)
     arrived(rows_got, S_PREV)
-    for h, at in enumerate(heads):
-        before_rows = jnp.where(block > 0, rows_got[:, at].astype(jnp.float32), 0.0)
-        upper = jnp.concatenate([ones[h][:64] + before_rows, ones[h][64:] + second[h]], axis=0)
-        attended[t, 0:128, at] = upper.astype(jnp.bfloat16)
-    to(piece(0, t), S_ATT + 2, (c, n, right))
-    to(piece(0, t), S_ATT + 3, (c, n, left))
+    leave(3, [after[h] + jnp.where(block > 0, rows_got[:, at].astype(jnp.float32), 0.0) for h, at in enumerate(heads)])
+    pass_on(2)
 
     out_right_in(3)
     for i in range(8):
@@ -363,21 +398,22 @@
         arrived(w_out.at[lax.rem(at, 8), 1 - core], S_OUT_MATE + i)
     own[9].wait()
 
-    def product(shard):
-        return dot(attended[shard], w_out[pl.ds(2 * shard, 2)].reshape(512, 1024), NN)
-
-    arrived(piece(1, left), S_ATT)
-    to(piece(1, left), S_ATT + 4, (c, n, right))
+    def product(shard, rows=slice(0, 256)):
+        return dot(attended[shard, rows], w_out[pl.ds(2 * shard, 2)].reshape(512, 1024), NN)
+
     total[...] = hidden[...].astype(jnp.float32) + product(t)
-    arrived(piece(0, right), S_ATT + 3)
-    to(piece(0, right), S_ATT + 5, (c, n, left))
-    arrived(piece(0, left), S_ATT + 2)
+    pass_on(3)
+    for i in (1, 3):
+        arrived(piece(i, left), S_ATT + 3 * i)
     total[...] += product(left)
-    arrived(piece(1, right), S_ATT + 1)
+    for i in (0, 2):
+        arrived(piece(i, right), S_ATT + 3 * i + 1)
     total[...] += product(right)
-    arrived(piece(1, across), S_ATT + 4)
-    arrived(piece(0, across), S_ATT + 5)
-    output[...] = (total[...] + product(across)).astype(jnp.bfloat16)
+    for half in range(2):
+        for i in (2 * half, 2 * half + 1):
+            arrived(piece(i, across), S_ATT + 3 * i + 2)
+        rows = slice(128 - 128 * half, 256 - 128 * half)
+        output[rows] = (total[rows] + product(across, rows)).astype(jnp.bfloat16)
 
     for k in range(2):
 
@@ -428,8 +464,10 @@
             pltpu.VMEM((64, 512), bf16),
             pltpu.VMEM((2, 128, 768), bf16),
             pltpu.VMEM((4, 192, 128), bf16),
-            pltpu.VMEM((3, 2, 192, 128), bf16),
-            pltpu.VMEM((4, 2, 192, 128), bf16),
+            pltpu.VMEM((2, 3, 192, 128), bf16),
+            pltpu.VMEM((2, 192, 128), bf16),
+            pltpu.VMEM((2, 3, 192, 128), bf16),
+            pltpu.VMEM((2, 192, 128), bf16),
             pltpu.VMEM((2, 4, 2, 96, 768), bf16),
             pltpu.VMEM((2, 128, 768), bf16),
             pltpu.VMEM((4, 192, 256), bf16),

time: 69 us -> 72 us (1.043)
  Pallas kernels: 66.9 us -> 70 us
    pallas_call x1, Pallas kernels: 66.9 us -> 70 us  [per_device(): pl.pallas_call(body, out_shape=jax.ShapeDtypeStruct((256, 1024), bf16), i...]
where the time goes in v3:
time: 72 us; the launch traced here: 71.8 us
  Pallas kernels  70 us (97%)
  local copies, waits for them, and re-layouts  1.87 us (3%)
    pallas_call x1, Pallas kernels, per_device(): pl.pallas_call(body, out_shape=jax.ShapeDtypeStruct((256, 1024), bf16), i...  70 us
    unnamed x1, local copies, waits for them, and re-layouts  1.87 us

profile of v3, /device:TPU:1, one launch (start us, length us, event | category | flops | bytes accessed | tf_op | source)
XLA Modules:
  0.0 71.8 jit_solution(2682206147663814827)
XLA Ops:
  0.0 70.0 %shard_map.145 = bf16[256,1024]{1,0:T(8,128)(2,1)} custom-call(s32[8,128]{1,0:T(8,128)} %bitcast.11, s32[4]{0:T(128)} %counts.1, bf16[8,128,768]{2,1,0:T(8,128)(2,1)} %embed.1, bf16[192,256]{1,0:T(8,128)(2,1)} %bitcast.9, bf16[192,256]{1,0:T(8,128)(2,1)} %bitcast.10, bf16[2,96,768]{2,1,0:T(8,128)(2,1)} %bitcast.7, bf16[2,96,768]{2,1,0:T(8,128)(2,1)} %bitcast.8, ...), custom_call_target="tpu_custom_call" | custom-call | flops 4000000000 | bytes 150000000 | tf_op jit(solution)/shard_map/pallas_call | solution.py:448
  70.0 1.9 %copy.17 = bf16[256,1024]{1,0:T(8,128)(2,1)} copy(bf16[256,1024]{1,0:T(8,128)(2,1)} %shard_map.145) | data formatting | bytes 1048576

commit v4 on v2

--- a/solution.py
+++ b/solution.py
@@ -18,8 +18,9 @@
 S_EMB, S_COND, S_ENC_W, S_KV_RIGHT, S_KV_LEFT, S_KV_MATE, S_QUERY, S_AG, S_PREV, S_ATT = (
     0, 2, 5, 13, 17, 20, 21, 22, 28, 29,
 )
-S_OUT_RIGHT, S_OUT_LEFT, S_OUT_MATE = 35, 39, 42
-N_SEMS = 50
+S_OUT_RIGHT, S_OUT_LEFT, S_OUT_MATE = 41, 45, 48
+S_COND_LAST = 56
+N_SEMS = 57
 
 
 def dot(a, b, dims):
@@ -36,7 +37,7 @@
     gain_in, gain_out,
     output,
     cond_k, cond_v, queries, ids, w_out, hidden, total, attended, queries_next, rows_send, rows_got,
-    emb, packs, cond_send, cond, enc_w, normed, mixed, encoded, kv_w, keys, values, key_mask, send, recv, local,
+    emb, packs, cond_send, cond_own, cond_side, cond_across, enc_w, normed, mixed, encoded, kv_w, keys, values, key_mask, send, recv, local, ready,
 ):
     c, n, t = lax.axis_index("ctx"), lax.axis_index("nbr"), lax.axis_index("tp")
     block = c * 8 + n
@@ -83,31 +84,57 @@
         made.start()
 
     barrier = pltpu.get_barrier_semaphore()
+    others = (first, first + 4)
+    mine = n // 4
+
+    def hello(device):
+        pl.semaphore_signal(barrier, inc=1, device_id=device, device_id_type=MESH)
+
+    def answer(i, device):
+        pl.semaphore_signal(ready.at[i], inc=1, device_id=device, device_id_type=MESH)
+
     for device in (
-        (c, n, right), (c, n, left), (c, n, across), (mate, n, t), (c_right, n, t), (c_left, n, t), before_device,
-        next_device,
+        (c, n, right), (c, n, left), (c, n, across), (mate, n, t), (c_right, n, t), (c_left, n, t),
     ):
-        pl.semaphore_signal(barrier, inc=1, device_id=device, device_id_type=MESH)
-    for k in range(2):
-        other = first + 4 * k
-
-        @pl.when(other != n)
-        def _():
-            pl.semaphore_signal(barrier, inc=1, device_id=(c, other, t), device_id_type=MESH)
-
-    with_self = jnp.where(lax.rem(2 * n, 4) == t, 1, 0)
-    pl.semaphore_wait(barrier, 10 - with_self)
-
-    mine = n // 4
+        hello(device)
+    lower = jnp.where(n > 0, 1, 0) + jnp.where(n == 7, 1, 0)
+    for other in others:
+        lower = lower + jnp.where(other < n, 1, 0)
+
+        @pl.when(other > n)
+        def _():
+            hello((c, other, t))
+
+    @pl.when(n < 7)
+    def _():
+        hello(next_device)
+
+    @pl.when(n == 0)
+    def _():
+        hello(before_device)
+
+    pl.semaphore_wait(barrier, 6 + lower)
+    for other in others:
+
+        @pl.when(other < n)
+        def _():
+            answer(mine, (c, other, t))
+
+    @pl.when(n > 0)
+    def _():
+        answer(2, before_device)
+
+    @pl.when(n == 7)
+    def _():
+        answer(3, next_device)
 
     def emb_copy(k):
         other = first + 4 * k
         return copy(embed.at[other], emb.at[mine], S_EMB + k, S_EMB + mine, (c, other, t))
 
-    for k in range(2):
-        other = first + 4 * k
-
-        @pl.when(other != n)
+    for k, other in enumerate(others):
+
+        @pl.when(other < n)
         def _():
             emb_copy(k).start()
 
@@ -151,22 +178,35 @@
 
     kv_right(0)
     kv_left(0)
+    for k, other in enumerate(others):
+
+        @pl.when(other > n)
+        def _():
+            pl.semaphore_wait(ready.at[k], 1)
+            emb_copy(k).start()
 
     own[4].wait()
     own[5].wait()
     for st in range(4):
         at = slice(st * STRETCH_TOKENS, (st + 1) * STRETCH_TOKENS)
         packs[st] = jnp.concatenate([cond_k[:, at], cond_v[:, at]], axis=1)
-    for d in (1, 3, 2):
-        target = lax.rem(t + d, 4)
-        start = lax.rem(target - n + 8, 4)
+    def pack_for(shard, k):
+        return packs[slots[lax.rem(shard - n + 8, 4) + 4 * k, block] // 2]
+
+    for side, device in enumerate((right, left)):
         for k in range(2):
-            cond_send[d - 1, k] = packs[slots[start + 4 * k, block] // 2]
-        to(cond_send.at[d - 1], S_COND + d - 1, (c, n, target), dst=cond.at[t])
+            cond_send[side, k] = pack_for(device, k)
+        cond_send[side, 2] = pack_for(across, side)
+        to(cond_send.at[side], S_COND + side, (c, n, device), dst=cond_side.at[side])
     for k in range(2):
-        cond[t, k] = packs[slots[first + 4 * k, block] // 2]
+        cond_own[k] = pack_for(t, k)
 
     own[6].wait()
+
+    @pl.when(n == 0)
+    def _():
+        pl.semaphore_wait(ready.at[3], 1)
+
     to(queries.at[pl.ds(0, STRETCH_TOKENS)], S_QUERY, before_device, dst=queries_next)
     own[8].wait()
     out_right(0)
@@ -192,6 +232,9 @@
     arrived(enc_w.at[:, right, core], S_ENC_W + 1)
     to(enc_w.at[1, right, core], S_ENC_W + 3, (c, n, left))
     to(enc_w.at[:, right, core], S_ENC_W + 5, (mate, n, t))
+    for side, device in enumerate((right, left)):
+        arrived(cond_side.at[side], S_COND + side)
+        to(cond_side.at[side, 2], (S_COND + 2, S_COND_LAST)[side], (c, n, device), dst=cond_across.at[side])
     kv_right_in(1)
     kv_right(2)
     kv_left_in(1)
@@ -210,7 +253,7 @@
 
         normed[k] = norm_rows(emb[k].astype(jnp.float32), gain_in[...].astype(jnp.float32).reshape(1, 768))
 
-    def encode_heads(shard):
+    def encode_heads(shard, states):
         query = dot(enc_w[0, shard].reshape(192, 768), normed[...].reshape(256, 768), NT)
         query = query.astype(jnp.bfloat16) * jnp.bfloat16(EHD ** (-0.5))
         columns = []
@@ -218,7 +261,7 @@
             rows = []
             for h in range(3):
                 at = slice(h * EHD, (h + 1) * EHD)
-                both = cond[shard, k, at, :]
+                both = states[k, at, :]
                 scores = dot(both, query[at, k * 128 : (k + 1) * 128], TN)[:STRETCH_TOKENS]
                 raised = jnp.exp(scores - jnp.max(scores, axis=0, keepdims=True))
                 weights = (raised / jnp.sum(raised, axis=0, keepdims=True)).astype(jnp.bfloat16)
@@ -227,7 +270,7 @@
             columns.append(jnp.concatenate(rows, axis=0))
         mixed[shard] = jnp.concatenate(columns, axis=1)
 
-    encode_heads(t)
+    encode_heads(t, cond_own)
     arrived(enc_w.at[0, across, core], S_ENC_W + 2)
     to(enc_w.at[0, across, core], S_ENC_W + 6, (mate, n, t))
     arrived(enc_w.at[1, across, core], S_ENC_W + 3)
@@ -236,18 +279,17 @@
     out_right(1)
     out_left_in(0)
     out_left(1)
-    arrived(cond.at[left], S_COND)
     arrived(enc_w.at[:, left, 1 - core], S_ENC_W + 4)
-    encode_heads(left)
+    encode_heads(left, cond_side.at[0])
     kv_right_in(2)
     kv_right(3)
     kv_left_in(2)
-    arrived(cond.at[right], S_COND + 2)
     arrived(enc_w.at[:, right, 1 - core], S_ENC_W + 5)
-    encode_heads(right)
-    arrived(cond.at[across], S_COND + 1)
+    encode_heads(right, cond_side.at[1])
+    for side in range(2):
+        arrived(cond_across.at[side], (S_COND + 2, S_COND_LAST)[side])
     arrived(enc_w.at[0, across, 1 - core], S_ENC_W + 6)
-    encode_heads(across)
+    encode_heads(across, cond_across)
     arrived(enc_w.at[1, across, 1 - core], S_ENC_W + 7)
 
     updated = dot(mixed[...].reshape(768, 256), enc_w[1].reshape(768, 768), TN)
@@ -332,30 +374,51 @@
         got = attend(3, h, jnp.concatenate([queries[192:256, at], queries_next[:, at]], axis=0))
         rows_send[:, at] = got[64:].astype(jnp.bfloat16)
         fourth.append(got[:64])
+
+    @pl.when(n < 7)
+    def _():
+        pl.semaphore_wait(ready.at[2], 1)
+
     to(rows_send, S_PREV, next_device, dst=rows_got)
 
-    second = []
-    for h, at in enumerate(heads):
-        three = attend(2, h, queries[128:256, at])
-        two = attend(1, h, queries[64:192, at])
-        lower = jnp.concatenate([two[64:] + three[:64], three[64:] + fourth[h]], axis=0)
-        attended[t, 128:256, at] = lower.astype(jnp.bfloat16)
-        second.append(two[:64])
-
-    def piece(half, shard):
-        return attended.at[shard, pl.ds(128 * half, 128)]
-
-    to(piece(1, t), S_ATT, (c, n, right))
-    to(piece(1, t), S_ATT + 1, (c, n, left))
-
-    ones = [attend(0, h, queries[0:128, at]) for h, at in enumerate(heads)]
+    def rows_of(shard, start, size):
+        return attended.at[shard, pl.ds(start, size)]
+
+    pieces = ((128, 128), (64, 64), (0, 64))
+
+    def leave(i, rows):
+        start, size = pieces[i]
+        for h, at in enumerate(heads):
+            attended[t, start : start + size, at] = rows[h].astype(jnp.bfloat16)
+        to(rows_of(t, start, size), S_ATT + 4 * i, (c, n, right))
+        to(rows_of(t, start, size), S_ATT + 4 * i + 1, (c, n, left))
+
+    def pass_on(i):
+        start, size = pieces[i]
+        arrived(rows_of(left, start, size), S_ATT + 4 * i)
+        to(rows_of(left, start, size // 2), S_ATT + 4 * i + 2, (c, n, right))
+        arrived(rows_of(right, start, size), S_ATT + 4 * i + 1)
+        to(rows_of(right, start + size // 2, size // 2), S_ATT + 4 * i + 3, (c, n, left))
+
+    def passed_on(i):
+        start, size = pieces[i]
+        arrived(rows_of(across, start, size // 2), S_ATT + 4 * i + 2)
+        arrived(rows_of(across, start + size // 2, size // 2), S_ATT + 4 * i + 3)
+
+    got = [[attend(st, h, queries[64 * st : 64 * st + 128, at]) for h, at in enumerate(heads)] for st in (2, 1)]
+    leave(
+        0,
+        [
+            jnp.concatenate([got[1][h][64:] + got[0][h][:64], got[0][h][64:] + fourth[h]], axis=0)
+            for h in range(4)
+        ],
+    )
+    zero = [attend(0, h, queries[0:128, at]) for h, at in enumerate(heads)]
+    leave(1, [zero[h][64:] + got[1][h][:64] for h in range(4)])
     arrived(rows_got, S_PREV)
-    for h, at in enumerate(heads):
-        before_rows = jnp.where(block > 0, rows_got[:, at].astype(jnp.float32), 0.0)
-        upper = jnp.concatenate([ones[h][:64] + before_rows, ones[h][64:] + second[h]], axis=0)
-        attended[t, 0:128, at] = upper.astype(jnp.bfloat16)
-    to(piece(0, t), S_ATT + 2, (c, n, right))
-    to(piece(0, t), S_ATT + 3, (c, n, left))
+    leave(2, [zero[h][:64] + jnp.where(block > 0, rows_got[:, at].astype(jnp.float32), 0.0) for h, at in enumerate(heads)])
+    pass_on(0)
+    pass_on(1)
 
     out_right_in(3)
     for i in range(8):
@@ -363,21 +426,16 @@
         arrived(w_out.at[lax.rem(at, 8), 1 - core], S_OUT_MATE + i)
     own[9].wait()
 
-    def product(shard):
-        return dot(attended[shard], w_out[pl.ds(2 * shard, 2)].reshape(512, 1024), NN)
-
-    arrived(piece(1, left), S_ATT)
-    to(piece(1, left), S_ATT + 4, (c, n, right))
+    def product(shard, rows=slice(0, 256)):
+        return dot(attended[shard, rows], w_out[pl.ds(2 * shard, 2)].reshape(512, 1024), NN)
+
     total[...] = hidden[...].astype(jnp.float32) + product(t)
-    arrived(piece(0, right), S_ATT + 3)
-    to(piece(0, right), S_ATT + 5, (c, n, left))
-    arrived(piece(0, left), S_ATT + 2)
-    total[...] += product(left)
-    arrived(piece(1, right), S_ATT + 1)
-    total[...] += product(right)
-    arrived(piece(1, across), S_ATT + 4)
-    arrived(piece(0, across), S_ATT + 5)
-    output[...] = (total[...] + product(across)).astype(jnp.bfloat16)
+    pass_on(2)
+    total[...] += product(left) + product(right)
+    for i, rows in ((0, slice(128, 256)), (1, None), (2, slice(0, 128))):
+        passed_on(i)
+        if rows is not None:
+            output[rows] = (total[rows] + product(across, rows)).astype(jnp.bfloat16)
 
     for k in range(2):
 
@@ -428,8 +486,10 @@
             pltpu.VMEM((64, 512), bf16),
             pltpu.VMEM((2, 128, 768), bf16),
             pltpu.VMEM((4, 192, 128), bf16),
-            pltpu.VMEM((3, 2, 192, 128), bf16),
-            pltpu.VMEM((4, 2, 192, 128), bf16),
+            pltpu.VMEM((2, 3, 192, 128), bf16),
+            pltpu.VMEM((2, 192, 128), bf16),
+            pltpu.VMEM((2, 3, 192, 128), bf16),
+            pltpu.VMEM((2, 192, 128), bf16),
             pltpu.VMEM((2, 4, 2, 96, 768), bf16),
             pltpu.VMEM((2, 128, 768), bf16),
             pltpu.VMEM((4, 192, 256), bf16),
@@ -441,6 +501,7 @@
             pltpu.SemaphoreType.DMA((N_SEMS,)),
             pltpu.SemaphoreType.DMA((N_SEMS,)),
             pltpu.SemaphoreType.DMA((11,)),
+            pltpu.SemaphoreType.REGULAR((4,)),
         ],
         compiler_params=pltpu.CompilerParams(
             collective_id=0, has_side_effects=True, vmem_limit_bytes=62 * 2**20

time: 69 us -> 67.8 us (0.983)
  Pallas kernels: 66.9 us -> 65.7 us
    pallas_call x1, Pallas kernels: 66.9 us -> 65.7 us  [per_device(): pl.pallas_call(body, out_shape=jax.ShapeDtypeStruct((256, 1024), bf16), i...]
where the time goes in v4:
time: 67.8 us; the launch traced here: 67.6 us
  Pallas kernels  65.7 us (97%)
  local copies, waits for them, and re-layouts  1.87 us (3%)
    pallas_call x1, Pallas kernels, per_device(): pl.pallas_call(body, out_shape=jax.ShapeDtypeStruct((256, 1024), bf16), i...  65.7 us
    unnamed x1, local copies, waits for them, and re-layouts  1.87 us

profile of v4, /device:TPU:1, one launch (start us, length us, event | category | flops | bytes accessed | tf_op | source)
XLA Modules:
  0.0 67.6 jit_solution(15965218239156419573)
XLA Ops:
  0.0 65.7 %shard_map.145 = bf16[256,1024]{1,0:T(8,128)(2,1)} custom-call(s32[8,128]{1,0:T(8,128)} %bitcast.11, s32[4]{0:T(128)} %counts.1, bf16[8,128,768]{2,1,0:T(8,128)(2,1)} %embed.1, bf16[192,256]{1,0:T(8,128)(2,1)} %bitcast.9, bf16[192,256]{1,0:T(8,128)(2,1)} %bitcast.10, bf16[2,96,768]{2,1,0:T(8,128)(2,1)} %bitcast.7, bf16[2,96,768]{2,1,0:T(8,128)(2,1)} %bitcast.8, ...), custom_call_target="tpu_custom_call" | custom-call | flops 4000000000 | bytes 150000000 | tf_op jit(solution)/shard_map/pallas_call | solution.py:470
  65.7 1.9 %copy.17 = bf16[256,1024]{1,0:T(8,128)(2,1)} copy(bf16[256,1024]{1,0:T(8,128)(2,1)} %shard_map.145) | data formatting | bytes 1048576

commit v5 on v4

--- a/solution.py
+++ b/solution.py
@@ -240,8 +240,8 @@
     kv_left_in(1)
     kv_left(2)
 
-    for k in range(2):
-        other = first + 4 * k
+    def take(k):
+        other = others[k]
 
         @pl.when(other != n)
         def _():
@@ -253,24 +253,29 @@
 
         normed[k] = norm_rows(emb[k].astype(jnp.float32), gain_in[...].astype(jnp.float32).reshape(1, 768))
 
-    def encode_heads(shard, states):
-        query = dot(enc_w[0, shard].reshape(192, 768), normed[...].reshape(256, 768), NT)
+    def encode_heads(shard, states, k):
+        query = dot(enc_w[0, shard].reshape(192, 768), normed[k], NT)
         query = query.astype(jnp.bfloat16) * jnp.bfloat16(EHD ** (-0.5))
-        columns = []
-        for k in range(2):
-            rows = []
-            for h in range(3):
-                at = slice(h * EHD, (h + 1) * EHD)
-                both = states[k, at, :]
-                scores = dot(both, query[at, k * 128 : (k + 1) * 128], TN)[:STRETCH_TOKENS]
-                raised = jnp.exp(scores - jnp.max(scores, axis=0, keepdims=True))
-                weights = (raised / jnp.sum(raised, axis=0, keepdims=True)).astype(jnp.bfloat16)
-                spread = jnp.concatenate([jnp.zeros_like(weights), weights], axis=0)
-                rows.append(dot(both, spread, NN).astype(jnp.bfloat16))
-            columns.append(jnp.concatenate(rows, axis=0))
-        mixed[shard] = jnp.concatenate(columns, axis=1)
-
-    encode_heads(t, cond_own)
+        rows = []
+        for h in range(3):
+            at = slice(h * EHD, (h + 1) * EHD)
+            both = states[k, at, :]
+            scores = dot(both, query[at], TN)[:STRETCH_TOKENS]
+            raised = jnp.exp(scores - jnp.max(scores, axis=0, keepdims=True))
+            weights = (raised / jnp.sum(raised, axis=0, keepdims=True)).astype(jnp.bfloat16)
+            spread = jnp.concatenate([jnp.zeros_like(weights), weights], axis=0)
+            rows.append(dot(both, spread, NN).astype(jnp.bfloat16))
+        mixed[k, shard] = jnp.concatenate(rows, axis=0)
+
+    def finish(k):
+        updated = dot(mixed[k].reshape(768, 128), enc_w[1].reshape(768, 768), TN)
+        rows = emb[k].astype(jnp.float32) + updated
+        encoded[first + 4 * k] = norm_rows(rows, gain_out[...].astype(jnp.float32).reshape(1, 768))
+        to(encoded.at[first + 4 * k], S_AG + 2 * k, (c, n, right))
+        to(encoded.at[first + 4 * k], S_AG + 2 * k + 1, (c, n, left))
+
+    take(0)
+    encode_heads(t, cond_own, 0)
     arrived(enc_w.at[0, across, core], S_ENC_W + 2)
     to(enc_w.at[0, across, core], S_ENC_W + 6, (mate, n, t))
     arrived(enc_w.at[1, across, core], S_ENC_W + 3)
@@ -280,27 +285,23 @@
     out_left_in(0)
     out_left(1)
     arrived(enc_w.at[:, left, 1 - core], S_ENC_W + 4)
-    encode_heads(left, cond_side.at[0])
+    encode_heads(left, cond_side.at[0], 0)
     kv_right_in(2)
     kv_right(3)
     kv_left_in(2)
     arrived(enc_w.at[:, right, 1 - core], S_ENC_W + 5)
-    encode_heads(right, cond_side.at[1])
+    encode_heads(right, cond_side.at[1], 0)
     for side in range(2):
         arrived(cond_across.at[side], (S_COND + 2, S_COND_LAST)[side])
     arrived(enc_w.at[0, across, 1 - core], S_ENC_W + 6)
-    encode_heads(across, cond_across)
+    encode_heads(across, cond_across, 0)
     arrived(enc_w.at[1, across, 1 - core], S_ENC_W + 7)
 
-    updated = dot(mixed[...].reshape(768, 256), enc_w[1].reshape(768, 768), TN)
-    gain = gain_out[...].astype(jnp.float32).reshape(1, 768)
-    for k in range(2):
-        rows = emb[k].astype(jnp.float32) + updated[k * 128 : (k + 1) * 128]
-        encoded[first + 4 * k] = norm_rows(rows, gain)
-
-    for k in range(2):
-        to(encoded.at[first + 4 * k], S_AG + 2 * k, (c, n, right))
-        to(encoded.at[first + 4 * k], S_AG + 2 * k + 1, (c, n, left))
+    finish(0)
+    take(1)
+    for shard, states in ((t, cond_own), (left, cond_side.at[0]), (right, cond_side.at[1]), (across, cond_across)):
+        encode_heads(shard, states, 1)
+    finish(1)
 
     kv_right_in(3)
     to(kv_w.at[:, :, core], S_KV_MATE, (mate, n, t))
@@ -492,7 +493,7 @@
             pltpu.VMEM((2, 192, 128), bf16),
             pltpu.VMEM((2, 4, 2, 96, 768), bf16),
             pltpu.VMEM((2, 128, 768), bf16),
-            pltpu.VMEM((4, 192, 256), bf16),
+            pltpu.VMEM((2, 4, 192, 128), bf16),
             pltpu.VMEM((8, 128, 768), bf16),
             pltpu.VMEM((2, 8, 2, 48, 512), bf16),
             pltpu.VMEM((8, 128, 512), bf16),

time: 67.8 us -> 65.6 us (0.968)
  Pallas kernels: 65.7 us -> 63.5 us
    pallas_call x1, Pallas kernels: 65.7 us -> 63.5 us  [per_device(): pl.pallas_call(body, out_shape=jax.ShapeDtypeStruct((256, 1024), bf16), i...]
where the time goes in v5:
time: 65.6 us; the launch traced here: 65.4 us
  Pallas kernels  63.5 us (97%)
  local copies, waits for them, and re-layouts  1.87 us (3%)
    pallas_call x1, Pallas kernels, per_device(): pl.pallas_call(body, out_shape=jax.ShapeDtypeStruct((256, 1024), bf16), i...  63.5 us
    unnamed x1, local copies, waits for them, and re-layouts  1.87 us

profile of v5, /device:TPU:1, one launch (start us, length us, event | category | flops | bytes accessed | tf_op | source)
XLA Modules:
  0.0 65.4 jit_solution(3733519803250368961)
XLA Ops:
  0.0 63.5 %shard_map.145 = bf16[256,1024]{1,0:T(8,128)(2,1)} custom-call(s32[8,128]{1,0:T(8,128)} %bitcast.11, s32[4]{0:T(128)} %counts.1, bf16[8,128,768]{2,1,0:T(8,128)(2,1)} %embed.1, bf16[192,256]{1,0:T(8,128)(2,1)} %bitcast.9, bf16[192,256]{1,0:T(8,128)(2,1)} %bitcast.10, bf16[2,96,768]{2,1,0:T(8,128)(2,1)} %bitcast.7, bf16[2,96,768]{2,1,0:T(8,128)(2,1)} %bitcast.8, ...), custom_call_target="tpu_custom_call" | custom-call | flops 4000000000 | bytes 150000000 | tf_op jit(solution)/shard_map/pallas_call | solution.py:471
  63.6 1.9 %copy.17 = bf16[256,1024]{1,0:T(8,128)(2,1)} copy(bf16[256,1024]{1,0:T(8,128)(2,1)} %shard_map.145) | data formatting | bytes 1048576

commit v6 on v5

--- a/solution.py
+++ b/solution.py
@@ -19,8 +19,8 @@
     0, 2, 5, 13, 17, 20, 21, 22, 28, 29,
 )
 S_OUT_RIGHT, S_OUT_LEFT, S_OUT_MATE = 41, 45, 48
-S_COND_LAST = 56
-N_SEMS = 57
+S_COND_LAST, S_AG_ON = 56, 57
+N_SEMS = 61
 
 
 def dot(a, b, dims):
@@ -328,19 +328,21 @@
         return lax.rem(shard - n + 8, 4)
 
     project_pair(first)
-    arrived(encoded.at[first_of(left)], S_AG)
-    to(encoded.at[first_of(left)], S_AG + 4, (c, n, right))
-    arrived(encoded.at[first_of(right) + 4], S_AG + 3)
-    to(encoded.at[first_of(right) + 4], S_AG + 5, (c, n, left))
-    arrived(encoded.at[first_of(left) + 4], S_AG + 2)
+    def half_of(shard, k, side):
+        return encoded.at[first_of(shard) + 4 * k, pl.ds(64 * side, 64)]
+
+    for k in range(2):
+        for side, (source, target) in enumerate(((left, right), (right, left))):
+            arrived(encoded.at[first_of(source) + 4 * k], S_AG + 2 * k + side)
+            to(half_of(source, k, side), S_AG_ON + 2 * k + side, (c, n, target))
     project_pair(first_of(left))
-    arrived(encoded.at[first_of(right)], S_AG + 1)
     project_pair(first_of(right))
     out_right_in(2)
     out_right(3)
     out_left_in(2)
-    arrived(encoded.at[first_of(across)], S_AG + 4)
-    arrived(encoded.at[first_of(across) + 4], S_AG + 5)
+    for k in range(2):
+        for side in range(2):
+            arrived(half_of(across, k, side), S_AG_ON + 2 * k + side)
 
     project_pair(first_of(across))
 

time: 65.6 us -> 65.7 us (level)
  no operation moved by 1% of the time
where the time goes in v6:
time: 65.7 us; the launch traced here: 65.5 us
  Pallas kernels  63.6 us (97%)
  local copies, waits for them, and re-layouts  1.87 us (3%)
    pallas_call x1, Pallas kernels, per_device(): pl.pallas_call(body, out_shape=jax.ShapeDtypeStruct((256, 1024), bf16), i...  63.6 us
    unnamed x1, local copies, waits for them, and re-layouts  1.87 us

profile of v6, /device:TPU:1, one launch (start us, length us, event | category | flops | bytes accessed | tf_op | source)
XLA Modules:
  0.0 65.5 jit_solution(12253186460818319766)
XLA Ops:
  0.0 63.6 %shard_map.145 = bf16[256,1024]{1,0:T(8,128)(2,1)} custom-call(s32[8,128]{1,0:T(8,128)} %bitcast.11, s32[4]{0:T(128)} %counts.1, bf16[8,128,768]{2,1,0:T(8,128)(2,1)} %embed.1, bf16[192,256]{1,0:T(8,128)(2,1)} %bitcast.9, bf16[192,256]{1,0:T(8,128)(2,1)} %bitcast.10, bf16[2,96,768]{2,1,0:T(8,128)(2,1)} %bitcast.7, bf16[2,96,768]{2,1,0:T(8,128)(2,1)} %bitcast.8, ...), custom_call_target="tpu_custom_call" | custom-call | flops 4000000000 | bytes 150000000 | tf_op jit(solution)/shard_map/pallas_call | solution.py:473
  63.6 1.9 %copy.17 = bf16[256,1024]{1,0:T(8,128)(2,1)} copy(bf16[256,1024]{1,0:T(8,128)(2,1)} %shard_map.145) | data formatting | bytes 1048576
